TPU v7x, 256 devices: a whole 4x4x8 slice. The times are simulated.
256 devices in a mesh: dp: 4 (over x), fsdp: 64 (over z, y, core).
Axes of the slice: x: 4, y: 4, z: 8, core: 2. Of those that a mesh axis runs over, the one named last changes fastest.
Arguments:
- grads: bfloat16 [4, 256, 512, 512], P('dp', None, 'fsdp'), may hold values from -32 to 32
- order: int32 [256], replicated, may hold values from 0 to 255, each once
- prev_roots: float32 [256, 2, 512, 512], P(('dp', 'fsdp')), may hold values from -1 to 3, as said below
Outputs:
- precond: bfloat16 [256, 512, 512], P(None, 'fsdp')
- new_roots: float32 [256, 2, 512, 512], P(('dp', 'fsdp'))
Inputs may be any that keep to these rules, and one draw needn't show every extreme that they name: `prev_roots`: each block is a symmetric matrix.
All inputs are finite; a program needn't handle non-finite values.
Results may differ from a plain program's by a relative error of at most 0.001.
Values may be sent and summed in bfloat16 or wider, within the bound.
No kernel may reach another device: no remote copies, remote signals or barrier semaphores. Data moves between devices by JAX's collectives and lax.ppermute only.
A program may use at most 128 MiB of HBM per device.

v0:
```python
import jax
import jax.numpy as jnp
from jax import lax
from jax.sharding import PartitionSpec as P

ITERS = 3


def product(left_side, right_side):
    return jnp.einsum(
        "...ij,...jk->...ik",
        left_side,
        right_side,
        precision=lax.Precision.HIGHEST,
        preferred_element_type=jnp.float32,
    )


def inverse_root(previous, statistic):
    width = statistic.shape[-1]
    frobenius = (
        jnp.sqrt(jnp.mean(statistic * statistic, axis=(-2, -1), keepdims=True) + 1e-06) * width
    )
    scaled = statistic / frobenius
    identity = jnp.eye(width, dtype=jnp.float32)
    square = product(previous, previous)
    fourth = product(square, square)
    moment = product(fourth, scaled)
    root = previous
    for step in range(ITERS):
        factor = (5.0 * identity - moment) * 0.25
        root = product(root, factor)
        if step + 1 < ITERS:
            factor_sq = product(factor, factor)
            moment = product(product(factor_sq, factor_sq), moment)
    return root


def body(grads, order, prev_roots):
    n_data = lax.axis_size("dp")
    n_owners = lax.axis_size("fsdp")
    local = grads[0]
    slots = prev_roots.shape[0]
    rows = local.shape[1]
    width = local.shape[2]
    owner_ids = jnp.transpose(order.reshape(n_data, n_owners, slots), (1, 0, 2)).reshape(-1)
    outgoing = jnp.take(local, owner_ids, axis=0)
    sectioned = outgoing.reshape(1, n_owners, n_data, slots, rows, width)
    arrived = lax.all_to_all(
        lax.all_to_all(sectioned, "dp", split_axis=2, concat_axis=0, tiled=True),
        "fsdp",
        split_axis=1,
        concat_axis=4,
        tiled=True,
    )
    arrived = arrived.reshape(n_data, slots, width, width)
    left_stat = jnp.einsum("dsij,dskj->sik", arrived, arrived, preferred_element_type=jnp.float32)
    right_stat = jnp.einsum("dsji,dsjk->sik", arrived, arrived, preferred_element_type=jnp.float32)
    mean_grad = jnp.sum(arrived, axis=0, dtype=jnp.float32) / n_data
    root_left = inverse_root(prev_roots[:, 0], left_stat)
    root_right = inverse_root(prev_roots[:, 1], right_stat)
    new_roots = jnp.stack([root_left, root_right], axis=1)
    refreshed = product(product(root_left, mean_grad), root_right).astype(jnp.bfloat16)
    positions = jnp.arange(order.shape[0], dtype=jnp.int32)
    owned = lax.all_gather(refreshed, "dp", axis=0, tiled=True)
    back = lax.all_to_all(
        owned.reshape(n_data * slots, n_owners, rows, width),
        "fsdp",
        split_axis=1,
        concat_axis=0,
        tiled=True,
    )
    back = back.reshape(n_owners * n_data * slots, rows, width)
    source_owner = positions // slots % n_owners
    source_data = positions // (n_owners * slots)
    lookup = source_owner * (n_data * slots) + source_data * slots + positions % slots
    inverse = jnp.zeros_like(order).at[order].set(positions)
    result = jnp.take(back, jnp.take(lookup, inverse, axis=0), axis=0)
    return (result, new_roots)


def solution(mesh):
    return jax.shard_map(
        body,
        mesh=mesh,
        in_specs=(P("dp", None, "fsdp", None), P(), P(("dp", "fsdp"), None, None, None)),
        out_specs=(P(None, "fsdp", None), P(("dp", "fsdp"), None, None, None)),
        check_vma=False,
    )
```

profile of v0, /device:TPU:1, one launch (start us, length us, event | category | flops | bytes accessed | tf_op | source)
XLA Modules:
  0.0 287.5 jit_solution(15225736792433441684)
XLA Ops:
  7.2 0.9 reshape.244
  8.8 2.1 gather_fusion.1
  10.8 2.1 broadcast_select_fusion.1
  13.0 1.2 copy.18
  14.2 29.9 %all_to_all.42 = bf16[1,64,4,1,8,512]{5,1,4,3,0,2:T(8,128)(2,1)S(1)} all-to-all(bf16[1,64,4,1,8,512]{5,1,4,3,0,2:T(8,128)(2,1)S(1)} %copy.18), channel_id=1, replica_groups=mesh['dp'=4,'fsdp'=64] {'dp'}, dimensions={2} | all-to-all | bytes 4194304 | tf_op jit(solution)/shard_map/all_to_all | solution.py:50
  44.1 2.5 copy.19
  46.6 13.8 %all-to-all-start.1 = ((bf16[4,64,1,1,8,512]{5,4,0,3,2,1:T(8,128)(2,1)}), bf16[4,64,1,1,8,512]{5,4,0,3,2,1:T(8,128)(2,1)}, u32[]{:S(2)}, u32[]{:S(2)}) async-start(bf16[4,64,1,1,8,512]{5,4,0,3,2,1:T(8,128)(2,1)} %copy.19), calls=%async_computation.1 | async-start | bytes 4194304 | tf_op jit(solution)/shard_map/all_to_all | solution.py:49
  60.7 3.5 %fusion.26 = f32[512,512]{1,0:T(8,128)S(1)} fusion(f32[1,2,512,512]{3,2,1,0:T(8,128)} %param.7), kind=kOutput, calls=%fused_computation.38 | convolution fusion | flops 1610612736 | bytes 2097152 | tf_op jit(solution)/shard_map/...ij,...jk->...ik/dot_general | solution.py:10
  64.3 1.8 fusion.20
  66.1 2.8 fusion.107
  68.9 2.8 fusion.112
  71.7 38.3 %all-to-all-done.1 = bf16[4,64,1,1,8,512]{5,4,0,3,2,1:T(8,128)(2,1)} async-done(((bf16[4,64,1,1,8,512]{5,4,0,3,2,1:T(8,128)(2,1)}), bf16[4,64,1,1,8,512]{5,4,0,3,2,1:T(8,128)(2,1)}, u32[]{:S(2)}, u32[]{:S(2)}) %all-to-all-start.1) | async-done | bytes 2097184 | tf_op jit(solution)/shard_map/all_to_all | solution.py:49
  110.0 5.1 %multiply_reduce_fusion.1 = (f32[]{:T(128)}, f32[512,512]{1,0:T(8,128)}) fusion(bf16[4,64,1,1,8,512]{5,4,0,3,2,1:T(8,128)(2,1)} %all-to-all-done.1), kind=kOutput, calls=%fused_computation.46 | convolution fusion | flops 1074266112 | bytes 3145732 | tf_op jit(solution)/shard_map/dsij,dskj->sik/dot_general | solution.py:57
  115.7 3.6 %fusion.31 = f32[512,512]{1,0:T(8,128)S(1)} fusion(f32[512,512]{1,0:T(8,128)} %fusion.107, f32[512,512]{1,0:T(8,128)} %get-tuple-element.6, f32[]{:T(128)S(6)} %mul.66), kind=kOutput, calls=%fused_computation.44 | convolution fusion | flops 1610874880 | bytes 3145732 | tf_op jit(solution)/shard_map/...ij,...jk->...ik/dot_general | solution.py:10
  119.3 4.9 %fusion.24 = f32[512,512]{1,0:T(8,128)} fusion(f32[1,2,512,512]{3,2,1,0:T(8,128)S(1)} %copy-done.4, f32[512,512]{1,0:T(8,128)S(1)} %fusion.31), kind=kOutput, calls=%fused_computation.36 | convolution fusion | flops 1611661312 | bytes 3145728 | tf_op jit(solution)/shard_map/...ij,...jk->...ik/dot_general | solution.py:10
  124.2 2.9 %fusion.48 = f32[512,512]{1,0:T(8,128)} fusion(f32[512,512]{1,0:T(8,128)S(1)} %fusion.31), kind=kOutput, calls=%fused_computation.57 | convolution fusion | flops 1611661312 | bytes 2097152 | tf_op jit(solution)/shard_map/...ij,...jk->...ik/dot_general | solution.py:10
  127.1 7.6 %multiply_reduce_fusion = (f32[]{:T(128)}, f32[512,512]{1,0:T(8,128)}) fusion(bf16[4,64,1,1,8,512]{5,4,0,3,2,1:T(8,128)(2,1)} %all-to-all-done.1), kind=kOutput, calls=%fused_computation.43 | convolution fusion | flops 1074266112 | bytes 3145732 | tf_op jit(solution)/shard_map/dsji,dsjk->sik/dot_general | solution.py:58
  135.3 3.6 %fusion.29 = f32[512,512]{1,0:T(8,128)S(1)} fusion(f32[512,512]{1,0:T(8,128)} %fusion.112, f32[512,512]{1,0:T(8,128)} %get-tuple-element.8, f32[]{:T(128)S(6)} %mul.71), kind=kOutput, calls=%fused_computation.41 | convolution fusion | flops 1610874880 | bytes 3145732 | tf_op jit(solution)/shard_map/...ij,...jk->...ik/dot_general | solution.py:10
  138.9 3.5 %fusion.18 = f32[512,512]{1,0:T(8,128)S(1)} fusion(f32[1,2,512,512]{3,2,1,0:T(8,128)S(1)} %copy-done.5, f32[512,512]{1,0:T(8,128)S(1)} %fusion.29), kind=kOutput, calls=%fused_computation.30 | convolution fusion | flops 1611661312 | bytes 3145728 | tf_op jit(solution)/shard_map/...ij,...jk->...ik/dot_general | solution.py:10
  142.4 2.1 fusion.41
  144.6 1.8 fusion.108
  146.4 1.8 fusion.109
  148.3 1.9 fusion.44
  150.2 1.9 fusion.46
  152.1 1.8 fusion.110
  154.0 1.9 fusion.12
  155.8 2.2 convert_reduce_fusion
  158.0 0.7 copy_multiply_fusion
  158.7 2.1 fusion.113
  160.8 1.8 fusion.114
  162.6 1.9 fusion.37
  164.6 2.0 fusion.39
  166.5 1.8 fusion.115
  168.4 1.9 fusion.13
  170.2 1.8 fusion.111
  172.1 2.6 fusion.22
  174.7 1.8 fusion.116
  176.6 1.0 copy-done.2
  177.6 2.6 convolution_convert_fusion
  180.2 29.3 %all-gather.3.cloned.1.call-done = bf16[2048,512]{1,0:T(8,128)(2,1)} async-done(((bf16[512,512]{1,0:T(8,128)(2,1)}), bf16[2048,512]{1,0:T(8,128)(2,1)}) %all-gather.3.cloned.1.call-update) | async-done | bytes 2097168 | tf_op jit(solution)/shard_map/all_gather | solution.py:65
  209.6 3.2 %copy.24 = bf16[4,64,8,512]{3,2,0,1:T(8,128)(2,1)} copy(bf16[4,64,8,512]{3,2,1,0:T(8,128)(2,1)} %bitcast.87) | data formatting | bytes 4194304 | tf_op jit(solution)/shard_map/reshape | solution.py:67
  212.8 11.0 %all-to-all-start.2 = ((bf16[4,64,8,512]{3,2,0,1:T(8,128)(2,1)}), bf16[4,64,8,512]{3,2,0,1:T(8,128)(2,1)}, u32[]{:S(2)}, u32[]{:S(2)}) async-start(bf16[4,64,8,512]{3,2,0,1:T(8,128)(2,1)} %copy.24), calls=%async_computation.2 | async-start | bytes 4194304 | tf_op jit(solution)/shard_map/all_to_all | solution.py:66
  223.8 1.4 scatter_custom_fusion
  225.3 1.9 gather_fusion
  227.3 2.7 pad_maximum_fusion
  230.0 43.4 %all-to-all-done.2 = bf16[4,64,8,512]{3,2,0,1:T(8,128)(2,1)} async-done(((bf16[4,64,8,512]{3,2,0,1:T(8,128)(2,1)}), bf16[4,64,8,512]{3,2,0,1:T(8,128)(2,1)}, u32[]{:S(2)}, u32[]{:S(2)}) %all-to-all-start.2) | async-done | bytes 2097184 | tf_op jit(solution)/shard_map/all_to_all | solution.py:66
  273.4 3.7 %gather_fusion.2 = bf16[256,8,512]{2,1,0:T(8,128)(2,1)} fusion(bf16[256,8,512]{2,1,0:T(8,128)(2,1)} %bitcast.18, s32[1024]{0:T(1024)S(1)} %pad_clamp_fusion), kind=kCustom, calls=%fused_computation.1.clone | custom fusion | bytes 4195328 | tf_op jit(solution)/shard_map/jit(_take)/gather | solution.py:78
  277.1 3.1 %broadcast_select_fusion = bf16[256,8,512]{2,1,0:T(8,128)(2,1)} fusion(bf16[256,8,512]{2,1,0:T(8,128)(2,1)} %gather_fusion.2, pred[256]{0:T(512)(128)(4,1)S(1)} %get-tuple-element.3), kind=kLoop, calls=%fused_computation.18 | loop fusion | flops 1048576 | bytes 4194560 | tf_op jit(solution)/shard_map/jit(_take)/select_n | solution.py:78
  (29 shorter events, 1.0 us)
Async XLA Ops:
  7.2 1.6 copy-start
  46.6 63.4 %all-to-all-start.1 = ((bf16[4,64,1,1,8,512]{5,4,0,3,2,1:T(8,128)(2,1)}), bf16[4,64,1,1,8,512]{5,4,0,3,2,1:T(8,128)(2,1)}, u32[]{:S(2)}, u32[]{:S(2)}) async-start(bf16[4,64,1,1,8,512]{5,4,0,3,2,1:T(8,128)(2,1)} %copy.19), calls=%async_computation.1 | async-start | bytes 4194304 | tf_op jit(solution)/shard_map/all_to_all | solution.py:49
  60.4 149.1 %all-gather.3.cloned.1.call-start = ((), (), s32[]{:S(2)}) async-start(), calls=%async_computation.3 | async-start | bytes 2621440 | tf_op jit(solution)/shard_map/all_gather | solution.py:65
  60.7 3.5 %copy-start.3 = (f32[1,2,512,512]{3,2,1,0:T(8,128)S(1)}, f32[1,2,512,512]{3,2,1,0:T(8,128)}, u32[]{:S(2)}) copy-start(f32[1,2,512,512]{3,2,1,0:T(8,128)} %param.7) | copy-start | bytes 6291460
  115.7 3.6 %copy-start.4 = (f32[1,2,512,512]{3,2,1,0:T(8,128)S(1)}, f32[1,2,512,512]{3,2,1,0:T(8,128)}, u32[]{:S(2)}) copy-start(f32[1,2,512,512]{3,2,1,0:T(8,128)} %param.7) | copy-start | bytes 6291460
  135.3 3.6 %copy-start.5 = (f32[1,2,512,512]{3,2,1,0:T(8,128)S(1)}, f32[1,2,512,512]{3,2,1,0:T(8,128)}, u32[]{:S(2)}) copy-start(f32[1,2,512,512]{3,2,1,0:T(8,128)} %param.7) | copy-start | bytes 6291460
  138.9 5.6 %copy-start.1 = (f32[512,512]{1,0:T(8,128)S(1)}, f32[512,512]{1,0:T(8,128)}, u32[]{:S(2)}) copy-start(f32[512,512]{1,0:T(8,128)} %fusion.48) | copy-start | bytes 3145732
  146.4 3.8 %copy-start.6 = (f32[512,512]{1,0:T(8,128)S(1)}, f32[512,512]{1,0:T(8,128)}, u32[]{:S(2)}) copy-start(f32[512,512]{1,0:T(8,128)} %fusion.24) | copy-start | bytes 3145732
  176.6 1.0 copy-start.2
  212.8 11.0 %copy-start.7 = (s32[256]{0:T(256)S(1)}, s32[256]{0:T(256)}, u32[]{:S(2)}) copy-start(s32[256]{0:T(256)} %param.6) | copy-start | bytes 3076
  212.8 60.6 %all-to-all-start.2 = ((bf16[4,64,8,512]{3,2,0,1:T(8,128)(2,1)}), bf16[4,64,8,512]{3,2,0,1:T(8,128)(2,1)}, u32[]{:S(2)}, u32[]{:S(2)}) async-start(bf16[4,64,8,512]{3,2,0,1:T(8,128)(2,1)} %copy.24), calls=%async_computation.2 | async-start | bytes 4194304 | tf_op jit(solution)/shard_map/all_to_all | solution.py:66
Sparse Core Ops, SparseCore 0:
  180.4 29.1 all-gather.2
where the time goes:
time: 292 us; the launch traced here: 287 us
  waiting for transfers between devices  111 us (38%)
  matrix products  75.8 us (26%)
  blocking collectives  29.9 us (10%)
  starting transfers between devices  25.1 us (9%)
  local copies, waits for them, and re-layouts  18.5 us (6%)
  between operations  16.1 us (6%)
  other arithmetic  10.9 us (4%)
    dot_general x26, matrix products, product(): jnp.einsum('...ij,...jk->...ik', left_side, right_side, precision=lax.Pre...  63.1 us
    all_to_all x1, waiting for transfers between devices, body(): lax.all_to_all(owned.reshape(n_data * slots, n_owners, rows, width), 'fsd...  43.4 us
    all_to_all x1, waiting for transfers between devices, body(): lax.all_to_all(lax.all_to_all(sectioned, 'dp', split_axis=2, concat_axis=...  38.3 us
    all_to_all x1, blocking collectives, body(): lax.all_to_all(sectioned, 'dp', split_axis=2, concat_axis=0, tiled=True)  29.9 us
    all_gather x1, waiting for transfers between devices, body(): owned = lax.all_gather(refreshed, 'dp', axis=0, tiled=True)  29.3 us
    all_to_all x1, starting transfers between devices, body(): lax.all_to_all(lax.all_to_all(sectioned, 'dp', split_axis=2, concat_axis=...  13.8 us
    all_to_all x1, starting transfers between devices, body(): lax.all_to_all(owned.reshape(n_data * slots, n_owners, rows, width), 'fsd...  11 us
    dot_general x1, matrix products, body(): jnp.einsum('dsji,dsjk->sik', arrived, arrived, preferred_element_type=jnp...  7.61 us
  transfers between devices with their start and end apart: 3, of which 3 were waited for; matrix products, arithmetic and copies ran while one was open for 6% of the time, Pallas kernels for 0%

commit v1 on v0

v1 whole, which is shorter than its diff:
```python
import jax
import jax.numpy as jnp
from jax import lax
from jax.sharding import PartitionSpec as P

ITERS = 3


def product(left_side, right_side):
    return jnp.einsum(
        "...ij,...jk->...ik",
        left_side,
        right_side,
        precision=lax.Precision.HIGH,
        preferred_element_type=jnp.float32,
    )


def inverse_root(previous, statistic):
    width = statistic.shape[-1]
    frobenius = (
        jnp.sqrt(jnp.mean(statistic * statistic, axis=(-2, -1), keepdims=True) + 1e-06) * width
    )
    scaled = statistic / frobenius
    identity = jnp.eye(width, dtype=jnp.float32)
    square = product(previous, previous)
    fourth = product(square, square)
    moment = product(fourth, scaled)
    root = previous
    for step in range(ITERS):
        factor = (5.0 * identity - moment) * 0.25
        root = product(root, factor)
        if step + 1 < ITERS:
            factor_sq = product(factor, factor)
            moment = product(product(factor_sq, factor_sq), moment)
    return root


def body(grads, order, prev_roots):
    n_data = lax.axis_size("dp")
    local = grads[0]
    width = local.shape[2]
    outgoing = local.at[order].get(mode="promise_in_bounds", unique_indices=True)
    arrived = lax.all_to_all(outgoing, ("dp", "fsdp"), split_axis=0, concat_axis=0, tiled=True)
    arrived = arrived.reshape(n_data, width, width)
    left_stat = jnp.einsum("dij,dkj->ik", arrived, arrived, preferred_element_type=jnp.float32)
    right_stat = jnp.einsum("dji,djk->ik", arrived, arrived, preferred_element_type=jnp.float32)
    mean_grad = jnp.sum(arrived, axis=0, dtype=jnp.float32) / n_data
    root_left = inverse_root(prev_roots[0, 0], left_stat)
    root_right = inverse_root(prev_roots[0, 1], right_stat)
    new_roots = jnp.stack([root_left, root_right], axis=0)[None]
    refreshed = product(product(root_left, mean_grad), root_right).astype(jnp.bfloat16)
    rows = local.shape[1]
    pieces = refreshed.reshape(width // rows, rows, width)
    mine = lax.all_to_all(pieces, "fsdp", split_axis=0, concat_axis=0, tiled=True)
    back = lax.all_gather(mine, "dp", axis=0, tiled=True)
    positions = jnp.arange(order.shape[0], dtype=jnp.int32)
    inverse = jnp.zeros_like(order).at[order].set(
        positions, mode="promise_in_bounds", unique_indices=True
    )
    result = back.at[inverse].get(mode="promise_in_bounds", unique_indices=True)
    return (result, new_roots)


def solution(mesh):
    return jax.shard_map(
        body,
        mesh=mesh,
        in_specs=(P("dp", None, "fsdp", None), P(), P(("dp", "fsdp"), None, None, None)),
        out_specs=(P(None, "fsdp", None), P(("dp", "fsdp"), None, None, None)),
        check_vma=False,
    )
```

time: 292 us -> 187 us (0.64); the launches traced: 287 us -> 187 us
  waiting for transfers between devices: 111 us -> 68.6 us
  matrix products: 75.8 us -> 47.9 us
  local copies, waits for them, and re-layouts: 18.5 us -> 8.89 us
  starting transfers between devices: 25.1 us -> 16.7 us
  blocking collectives: 29.9 us -> 23.4 us
  other arithmetic: 10.9 us -> 5.57 us
    all_to_all x2 -> x1, waiting for transfers between devices: 81.7 us -> 44.7 us  [body(): lax.all_to_all(outgoing, ('dp', 'fsdp'), split_axis=0, concat_axis=0, til...]
    dot_general x26, matrix products: 63.1 us -> 37.8 us  [product(): jnp.einsum('...ij,...jk->...ik', left_side, right_side, precision=lax.Pre...]
    all_to_all x2 -> x1, starting transfers between devices: 24.8 us -> 16.7 us  [body(): lax.all_to_all(outgoing, ('dp', 'fsdp'), split_axis=0, concat_axis=0, til...]
    all_to_all x1, blocking collectives: 29.9 us -> 23.4 us  [body(): lax.all_to_all(pieces, 'fsdp', split_axis=0, concat_axis=0, tiled=True)]
    all_gather x1, waiting for transfers between devices: 29.3 us -> 23.9 us  [body(): back = lax.all_gather(mine, 'dp', axis=0, tiled=True)]
    reshape x4 -> x0, local copies, waits for them, and re-layouts: 5.4 us -> none  [the longest x1 3.22 us: body(): owned.reshape(n_data * slots, n_owners, rows, width)]
    select_n x5 -> x2, other arithmetic: 5.25 us -> 0.83 us  [the longest x1 0.83 us: body(): local.at[order].get(mode='promise_in_bounds', unique_indices=True)]
    gather x3 -> x2, local copies, waits for them, and re-layouts: 7.68 us -> 5.73 us  [the longest x1 3.66 us: body(): result = back.at[inverse].get(mode='promise_in_bounds', unique_indices=True)]
  transfers between devices with their start and end apart: 3 -> 2, of which waited for: 3 -> 2; matrix products, arithmetic and copies ran while one was open for 6% -> 6% of each run, Pallas kernels for 0% -> 0%
where the time goes in v1:
time: 187 us
  waiting for transfers between devices  68.6 us (37%)
  matrix products  47.9 us (26%)
  blocking collectives  23.4 us (13%)
  starting transfers between devices  16.7 us (9%)
  between operations  15.5 us (8%)
  local copies, waits for them, and re-layouts  8.89 us (5%)
  other arithmetic  5.57 us (3%)
    all_to_all x1, waiting for transfers between devices, body(): lax.all_to_all(outgoing, ('dp', 'fsdp'), split_axis=0, concat_axis=0, til...  44.7 us
    dot_general x26, matrix products, product(): jnp.einsum('...ij,...jk->...ik', left_side, right_side, precision=lax.Pre...  37.8 us
    all_gather x1, waiting for transfers between devices, body(): back = lax.all_gather(mine, 'dp', axis=0, tiled=True)  23.9 us
    all_to_all x1, blocking collectives, body(): lax.all_to_all(pieces, 'fsdp', split_axis=0, concat_axis=0, tiled=True)  23.4 us
    all_to_all x1, starting transfers between devices, body(): lax.all_to_all(outgoing, ('dp', 'fsdp'), split_axis=0, concat_axis=0, til...  16.7 us
    dot_general x1, matrix products, body(): jnp.einsum('dji,djk->ik', arrived, arrived, preferred_element_type=jnp.fl...  5.09 us
    dot_general x1, matrix products, body(): jnp.einsum('dij,dkj->ik', arrived, arrived, preferred_element_type=jnp.fl...  5.04 us
  transfers between devices with their start and end apart: 2, of which 2 were waited for; matrix products, arithmetic and copies ran while one was open for 6% of the time, Pallas kernels for 0%

profile of v1, /device:TPU:1, one launch (start us, length us, event | category | flops | bytes accessed | tf_op | source)
XLA Modules:
  0.0 186.6 jit_solution(15248726684604175443)
XLA Ops:
  7.2 0.0 copy-start
  7.2 0.8 compare_select_fusion.1
  8.0 0.8 copy-done
  8.8 2.1 %gather_fusion = bf16[256,8,512]{2,1,0:T(8,128)(2,1)} fusion(bf16[256,8,512]{2,1,0:T(8,128)(2,1)S(1)} %bitcast.59, s32[1024]{0:T(1024)S(1)} %pad_clamp_fusion.1), kind=kCustom, calls=%fused_computation | custom fusion | bytes 4195328 | tf_op jit(solution)/shard_map/gather | solution.py:43
  10.8 16.7 %all-to-all-start = ((bf16[256,8,512]{2,1,0:T(8,128)(2,1)}), bf16[256,8,512]{2,1,0:T(8,128)(2,1)}, u32[]{:S(2)}, u32[]{:S(2)}) async-start(bf16[256,8,512]{2,1,0:T(8,128)(2,1)} %gather_fusion), calls=%async_computation | async-start | bytes 4194304 | tf_op jit(solution)/shard_map/all_to_all | solution.py:44
  27.5 0.0 all-gather.2.cloned.1.call-start
  27.6 0.0 copy-start.3
  27.6 2.7 %fusion.13 = f32[512,512]{1,0:T(8,128)S(1)} fusion(f32[1,2,512,512]{3,2,1,0:T(8,128)} %param.5), kind=kOutput, calls=%fused_computation.27 | convolution fusion | flops 805306368 | bytes 2097152 | tf_op jit(solution)/shard_map/...ij,...jk->...ik/dot_general | solution.py:10
  30.3 1.0 fusion.9
  31.3 2.0 %fusion.93 = f32[512,512]{1,0:T(8,128)} fusion(f32[512,512]{1,0:T(8,128)S(1)} %fusion.13), kind=kOutput, calls=%fused_computation.106 | convolution fusion | flops 805306368 | bytes 2097152 | tf_op jit(solution)/shard_map/...ij,...jk->...ik/dot_general | solution.py:10
  33.3 2.0 %fusion.98 = f32[512,512]{1,0:T(8,128)} fusion(f32[512,512]{1,0:T(8,128)S(1)} %fusion.9), kind=kOutput, calls=%fused_computation.111 | convolution fusion | flops 805306368 | bytes 2097152 | tf_op jit(solution)/shard_map/...ij,...jk->...ik/dot_general | solution.py:10
  35.3 44.7 %all-to-all-done = bf16[256,8,512]{2,1,0:T(8,128)(2,1)} async-done(((bf16[256,8,512]{2,1,0:T(8,128)(2,1)}), bf16[256,8,512]{2,1,0:T(8,128)(2,1)}, u32[]{:S(2)}, u32[]{:S(2)}) %all-to-all-start) | async-done | bytes 2097184 | tf_op jit(solution)/shard_map/all_to_all | solution.py:44
  80.0 5.0 %multiply_reduce_fusion.1 = (f32[]{:T(128)}, f32[512,512]{1,0:T(8,128)}) fusion(bf16[4,512,512]{2,1,0:T(8,128)(2,1)} %bitcast.2), kind=kOutput, calls=%fused_computation.36 | convolution fusion | flops 1074266112 | bytes 3145732 | tf_op jit(solution)/shard_map/dij,dkj->ik/dot_general | solution.py:46
  85.7 0.0 copy-start.4
  85.7 2.7 %fusion.19 = f32[512,512]{1,0:T(8,128)S(1)} fusion(f32[512,512]{1,0:T(8,128)} %fusion.93, f32[512,512]{1,0:T(8,128)} %get-tuple-element.3, f32[]{:T(128)S(6)} %mul.52), kind=kOutput, calls=%fused_computation.34 | convolution fusion | flops 805568512 | bytes 3145732 | tf_op jit(solution)/shard_map/...ij,...jk->...ik/dot_general | solution.py:10
  88.4 2.8 %fusion.11 = f32[512,512]{1,0:T(8,128)} fusion(f32[1,2,512,512]{3,2,1,0:T(8,128)S(1)} %copy-done.4, f32[512,512]{1,0:T(8,128)S(1)} %fusion.19), kind=kOutput, calls=%fused_computation.25 | convolution fusion | flops 806354944 | bytes 3145728 | tf_op jit(solution)/shard_map/...ij,...jk->...ik/dot_general | solution.py:10
  91.2 2.0 %fusion.36 = f32[512,512]{1,0:T(8,128)} fusion(f32[512,512]{1,0:T(8,128)S(1)} %fusion.19), kind=kOutput, calls=%fused_computation.47 | convolution fusion | flops 806354944 | bytes 2097152 | tf_op jit(solution)/shard_map/...ij,...jk->...ik/dot_general | solution.py:10
  93.2 5.1 %multiply_reduce_fusion = (f32[]{:T(128)}, f32[512,512]{1,0:T(8,128)}) fusion(bf16[256,8,512]{2,1,0:T(8,128)(2,1)} %all-to-all-done), kind=kOutput, calls=%fused_computation.31 | convolution fusion | flops 1074266112 | bytes 3145732 | tf_op jit(solution)/shard_map/dji,djk->ik/dot_general | solution.py:47
  98.9 0.0 copy-start.5
  98.9 2.7 %fusion.15 = f32[512,512]{1,0:T(8,128)S(1)} fusion(f32[512,512]{1,0:T(8,128)} %fusion.98, f32[512,512]{1,0:T(8,128)} %get-tuple-element.5, f32[]{:T(128)S(6)} %mul.57), kind=kOutput, calls=%fused_computation.29 | convolution fusion | flops 805568512 | bytes 3145732 | tf_op jit(solution)/shard_map/...ij,...jk->...ik/dot_general | solution.py:10
  101.7 2.1 %fusion.7 = f32[512,512]{1,0:T(8,128)S(1)} fusion(f32[1,2,512,512]{3,2,1,0:T(8,128)S(1)} %copy-done.5, f32[512,512]{1,0:T(8,128)S(1)} %fusion.15), kind=kOutput, calls=%fused_computation.21 | convolution fusion | flops 806354944 | bytes 3145728 | tf_op jit(solution)/shard_map/...ij,...jk->...ik/dot_general | solution.py:10
  103.7 1.1 fusion.29
  104.8 1.0 fusion.94
  105.9 0.0 copy-start.6
  105.9 1.0 fusion.95
  106.9 1.0 fusion.32
  108.0 1.0 fusion.34
  109.0 1.0 fusion.96
  110.0 1.0 fusion
  111.0 2.0 %convert_reduce_fusion = f32[512,512]{1,0:T(8,128)S(1)} fusion(bf16[4,512,512]{2,1,0:T(8,128)(2,1)} %bitcast.58), kind=kLoop, calls=%fused_computation.3 | loop fusion | flops 1835008 | bytes 3145728 | tf_op jit(solution)/shard_map/reduce_sum | solution.py:48
  113.1 1.0 fusion.99
  114.1 1.0 fusion.100
  115.2 1.1 fusion.25
  116.2 1.3 fusion.27
  117.5 1.0 fusion.101
  118.5 1.0 fusion.1
  119.6 1.0 fusion.97
  120.6 1.0 fusion.17
  121.7 1.0 fusion.102
  122.7 0.0 copy-start.2
  122.7 1.0 copy-done.2
  123.7 1.0 fusion.2
  124.7 23.4 %all_to_all.10 = bf16[64,8,512]{2,1,0:T(8,128)(2,1)} all-to-all(bf16[64,8,512]{2,1,0:T(8,128)(2,1)S(1)} %fusion.2), channel_id=1, replica_groups=mesh['dp'=4,'fsdp'=64] {'fsdp'}, dimensions={0} | all-to-all | bytes 1048576 | tf_op jit(solution)/shard_map/all_to_all | solution.py:55
  148.0 0.0 all-gather.2.cloned.1.call-update
  148.1 1.4 scatter_custom_fusion
  149.5 2.7 %maximum_bitcast_fusion = f32[1,2,512,512]{3,2,1,0:T(8,128)} fusion(f32[1,512,512]{2,1,0:T(8,128)} %bitcast.61, f32[1,512,512]{2,1,0:T(8,128)S(1)} %bitcast.60), kind=kLoop, calls=%fused_computation.10 | loop fusion | flops 524288 | bytes 4194304 | tf_op jit(solution)/shard_map/broadcast_in_dim | solution.py:51
  152.2 23.9 %all-gather.2.cloned.1.call-done = bf16[256,8,512]{2,1,0:T(8,128)(2,1)} async-done(((bf16[64,8,512]{2,1,0:T(8,128)(2,1)}), bf16[256,8,512]{2,1,0:T(8,128)(2,1)}) %all-gather.2.cloned.1.call-update) | async-done | bytes 2097168 | tf_op jit(solution)/shard_map/all_gather | solution.py:56
  176.1 3.7 %gather_fusion.1 = bf16[256,8,512]{2,1,0:T(8,128)(2,1)} fusion(bf16[256,8,512]{2,1,0:T(8,128)(2,1)} %all-gather.2.cloned.1.call-done, s32[1024]{0:T(1024)S(1)} %pad_clamp_fusion), kind=kCustom, calls=%fused_computation.1 | custom fusion | bytes 4195328 | tf_op jit(solution)/shard_map/gather | solution.py:61
  (10 shorter events, 0.0 us)
Async XLA Ops:
  7.2 1.6 copy-start
  10.8 69.2 %all-to-all-start = ((bf16[256,8,512]{2,1,0:T(8,128)(2,1)}), bf16[256,8,512]{2,1,0:T(8,128)(2,1)}, u32[]{:S(2)}, u32[]{:S(2)}) async-start(bf16[256,8,512]{2,1,0:T(8,128)(2,1)} %gather_fusion), calls=%async_computation | async-start | bytes 4194304 | tf_op jit(solution)/shard_map/all_to_all | solution.py:44
  27.5 148.6 %all-gather.2.cloned.1.call-start = ((), (), s32[]{:S(2)}) async-start(), calls=%async_computation.2 | async-start | bytes 2621440 | tf_op jit(solution)/shard_map/all_gather | solution.py:56
  27.6 2.7 %copy-start.3 = (f32[1,2,512,512]{3,2,1,0:T(8,128)S(1)}, f32[1,2,512,512]{3,2,1,0:T(8,128)}, u32[]{:S(2)}) copy-start(f32[1,2,512,512]{3,2,1,0:T(8,128)} %param.5) | copy-start | bytes 6291460
  85.7 2.7 %copy-start.4 = (f32[1,2,512,512]{3,2,1,0:T(8,128)S(1)}, f32[1,2,512,512]{3,2,1,0:T(8,128)}, u32[]{:S(2)}) copy-start(f32[1,2,512,512]{3,2,1,0:T(8,128)} %param.5) | copy-start | bytes 6291460
  98.9 2.7 %copy-start.5 = (f32[1,2,512,512]{3,2,1,0:T(8,128)S(1)}, f32[1,2,512,512]{3,2,1,0:T(8,128)}, u32[]{:S(2)}) copy-start(f32[1,2,512,512]{3,2,1,0:T(8,128)} %param.5) | copy-start | bytes 6291460
  101.7 3.1 %copy-start.1 = (f32[512,512]{1,0:T(8,128)S(1)}, f32[512,512]{1,0:T(8,128)}, u32[]{:S(2)}) copy-start(f32[512,512]{1,0:T(8,128)} %fusion.36) | copy-start | bytes 3145732
  105.9 2.1 %copy-start.6 = (f32[512,512]{1,0:T(8,128)S(1)}, f32[512,512]{1,0:T(8,128)}, u32[]{:S(2)}) copy-start(f32[512,512]{1,0:T(8,128)} %fusion.11) | copy-start | bytes 3145732
  122.7 1.0 copy-start.2
Sparse Core Ops, SparseCore 0:
  148.2 27.8 all-gather.1

commit v2 on v1

v2 whole, which is shorter than its diff:
```python
import functools

import jax
import jax.numpy as jnp
from jax import lax
from jax.experimental import pallas as pl
from jax.experimental.pallas import tpu as pltpu
from jax.sharding import PartitionSpec as P

ITERS = 3
MB = 1 << 20
BF16 = jnp.bfloat16
F32 = jnp.float32
ANY = pl.BlockSpec(memory_space=pl.ANY)
VMEM = pl.BlockSpec(memory_space=pltpu.VMEM)
SMEM = pl.BlockSpec(memory_space=pltpu.SMEM)


def split(value):
    high = value.astype(BF16)
    return high, (value - high.astype(F32)).astype(BF16)


def product3(lhs, rhs, rows):
    high = lhs[0, rows, :]
    left = jnp.concatenate([high, lhs[1, rows, :], high], axis=1)
    over = rhs[0]
    right = jnp.concatenate([over, over, rhs[1]], axis=0)
    return jnp.dot(left, right, preferred_element_type=F32)


def keep(target, rows, value):
    high, low = split(value)
    target[0, rows, :] = high
    target[1, rows, :] = low


def halves(width):
    size = width // 2
    return [pl.ds(0, size), pl.ds(size, size)]


def fourth_kernel(prev, x_out, q_out, square):
    width = prev.shape[-1]
    for side in range(2):
        keep(x_out.at[side], slice(None), prev[side])
    for source, target in ((x_out, square), (square, q_out)):
        for rows in halves(width):
            for side in range(2):
                keep(target.at[side], rows, product3(source.at[side], source.at[side], rows))


def fourth_powers(prev):
    width = prev.shape[-1]
    pair = jax.ShapeDtypeStruct((2, 2, width, width), BF16)
    return pl.pallas_call(
        fourth_kernel,
        out_shape=(pair, pair),
        in_specs=[VMEM],
        out_specs=(VMEM, VMEM),
        scratch_shapes=[pltpu.VMEM((2, 2, width, width), BF16)],
        compiler_params=pltpu.CompilerParams(vmem_limit_bytes=20 * MB),
        cost_estimate=pl.CostEstimate(
            flops=2 * 2 * 3 * 2 * width**3, bytes_accessed=6 * MB, transcendentals=0
        ),
        name="fourth_powers",
    )(prev)


def refresh_kernel(
    arrived, x, q, roots, out, stat, moment, factor, power, root, mean, mixed
):
    n_micro, width = arrived.shape[0], arrived.shape[-1]
    parts = halves(width)
    size = width // 2
    scales = []
    whole = [arrived[d] for d in range(n_micro)]
    for side in range(2):
        total = jnp.zeros((1, 1), F32)
        if side == 0:
            rhs = jnp.concatenate(whole, axis=1)
            contract = (((1,), (1,)), ((), ()))
        else:
            rhs = jnp.concatenate(whole, axis=0)
            contract = (((0,), (0,)), ((), ()))
        for index, rows in enumerate(parts):
            lo = index * size
            hi = lo + size
            lhs = rhs[lo:hi, :] if side == 0 else rhs[:, lo:hi]
            value = lax.dot_general(lhs, rhs, contract, preferred_element_type=F32)
            total = total + jnp.sum(value * value, axis=(0, 1), keepdims=True)
            keep(stat.at[side], rows, value)
        scales.append(1.0 / (jnp.sqrt(total / (width * width) + 1e-06) * width))
    for index, rows in enumerate(parts):
        lo = index * size
        value = whole[0][lo : lo + size].astype(F32)
        for d in range(1, n_micro):
            value = value + whole[d][lo : lo + size].astype(F32)
        keep(mean, rows, value / n_micro)

    row_ids = lax.broadcasted_iota(jnp.int32, (size, width), 0)
    col_ids = lax.broadcasted_iota(jnp.int32, (size, width), 1)

    def keep_factor(side, index, rows, value):
        diagonal = jnp.where(row_ids + index * size == col_ids, 1.25, 0.0)
        keep(factor.at[side], rows, diagonal - 0.25 * value)

    for index, rows in enumerate(parts):
        for side in range(2):
            value = product3(q.at[side], stat.at[side], rows) * scales[side]
            keep(moment.at[0, side], rows, value)
            keep_factor(side, index, rows, value)
    held = x
    for step in range(ITERS - 1):
        for rows in parts:
            for side in range(2):
                keep(
                    power.at[0, side], rows, product3(factor.at[side], factor.at[side], rows)
                )
        for rows in parts:
            for side in range(2):
                keep(
                    root.at[step % 2, side], rows, product3(held.at[side], factor.at[side], rows)
                )
        held = root.at[step % 2]
        for rows in parts:
            for side in range(2):
                keep(
                    power.at[1, side],
                    rows,
                    product3(power.at[0, side], power.at[0, side], rows),
                )
        for index, rows in enumerate(parts):
            for side in range(2):
                value = product3(power.at[1, side], moment.at[step % 2, side], rows)
                if step + 2 < ITERS:
                    keep(moment.at[(step + 1) % 2, side], rows, value)
                keep_factor(side, index, rows, value)
    final = root.at[(ITERS - 1) % 2]
    for side in range(2):
        for rows in parts:
            value = product3(held.at[side], factor.at[side], rows)
            roots[side, rows, :] = value
            keep(final.at[side], rows, value)
    for rows in parts:
        keep(mixed, rows, product3(final.at[0], mean, rows))
    for rows in parts:
        out[rows, :] = product3(mixed, final.at[1], rows).astype(BF16)


def refresh(arrived, x, q):
    width = arrived.shape[-1]
    matrix = (2, 2, width, width)
    return pl.pallas_call(
        refresh_kernel,
        out_shape=(
            jax.ShapeDtypeStruct((2, width, width), F32),
            jax.ShapeDtypeStruct((width, width), BF16),
        ),
        in_specs=[VMEM, VMEM, VMEM],
        out_specs=(VMEM, VMEM),
        scratch_shapes=[
            pltpu.VMEM(matrix, BF16),
            pltpu.VMEM((2,) + matrix, BF16),
            pltpu.VMEM(matrix, BF16),
            pltpu.VMEM((2,) + matrix, BF16),
            pltpu.VMEM((2,) + matrix, BF16),
            pltpu.VMEM((2, width, width), BF16),
            pltpu.VMEM((2, width, width), BF16),
        ],
        compiler_params=pltpu.CompilerParams(vmem_limit_bytes=36 * MB),
        cost_estimate=pl.CostEstimate(
            flops=(22 * 3 + 8) * 2 * width**3, bytes_accessed=9 * MB, transcendentals=0
        ),
        name="refresh_roots",
    )(arrived, x, q)


def place_kernel(owners, offset, order, source, *rest):
    out, sem = rest[-2:]
    blocks = source.shape[0]
    base = lax.rem(lax.axis_index("dp") + offset[0], lax.axis_size("dp")) * owners + offset[1]

    def step(i, _):
        pltpu.make_async_copy(source.at[i], out.at[order[base + i]], sem).start()
        return 0

    lax.fori_loop(0, blocks, step, 0, unroll=8)
    pltpu.make_async_copy(source, out.at[pl.ds(0, blocks)], sem).wait()


def place(owners, offset, order, source, base):
    rows, width = source.shape[1:]
    args, specs, aliases = [order, source], [SMEM, VMEM], {}
    if base is not None:
        args.append(base)
        specs.append(ANY)
        aliases = {2: 0}
    return pl.pallas_call(
        functools.partial(place_kernel, owners, offset),
        out_shape=jax.ShapeDtypeStruct((order.shape[0], rows, width), source.dtype),
        in_specs=specs,
        out_specs=ANY,
        scratch_shapes=[pltpu.SemaphoreType.DMA(())],
        input_output_aliases=aliases,
        compiler_params=pltpu.CompilerParams(vmem_limit_bytes=8 * MB),
        cost_estimate=pl.CostEstimate(
            flops=0, bytes_accessed=4 * source.size, transcendentals=0
        ),
        name="place_blocks",
    )(*args)


def body(grads, order, prev_roots):
    n_data = lax.axis_size("dp")
    local = grads[0]
    rows, width = local.shape[1:]
    outgoing = local.at[order].get(
        mode="promise_in_bounds", unique_indices=True, wrap_negative_indices=False
    )
    arrived = lax.all_to_all(outgoing, ("dp", "fsdp"), split_axis=0, concat_axis=0, tiled=True)
    x, q = fourth_powers(prev_roots[0])
    roots, refreshed = refresh(arrived.reshape(n_data, width, width), x, q)
    pieces = refreshed.reshape(width // rows, rows, width)
    mine = lax.all_to_all(pieces, "fsdp", split_axis=0, concat_axis=0, tiled=True)
    owners = mine.shape[0]
    half = owners // 2

    def shift(value, by):
        return lax.ppermute(value, "dp", [(i, (i + by) % n_data) for i in range(n_data)])

    low, high = mine[:half], mine[half:]
    low_up, high_down = shift(low, 1), shift(high, -1)
    high_up, low_down = shift(high, 1), shift(low, -1)
    low_far, high_far = shift(low_up, 1), shift(high_down, -1)
    result = None
    for offset, piece in (
        ((0, 0), mine),
        ((n_data - 1, 0), low_up),
        ((1, half), high_down),
        ((n_data - 1, half), high_up),
        ((1, 0), low_down),
        ((n_data - 2, 0), low_far),
        ((2, half), high_far),
    ):
        result = place(owners, offset, order, piece, result)
    return (result, roots[None])


def solution(mesh):
    return jax.shard_map(
        body,
        mesh=mesh,
        in_specs=(P("dp", None, "fsdp", None), P(), P(("dp", "fsdp"), None, None, None)),
        out_specs=(P(None, "fsdp", None), P(("dp", "fsdp"), None, None, None)),
        check_vma=False,
    )
```

time: 187 us -> 146 us (0.78)
  matrix products: 47.9 us -> 0 us
  Pallas kernels: 0 us -> 35 us
  waiting for transfers between devices: 68.6 us -> 50.1 us
  between operations: 15.5 us -> 0.93 us
  starting transfers between devices: 16.7 us -> 24.8 us
  other arithmetic: 5.57 us -> 0.83 us
    dot_general x28 -> x0, matrix products: 47.9 us -> none  [the longest x26 37.8 us: product(): jnp.einsum('...ij,...jk->...ik', left_side, right_side, precision=lax.Pre...]
    pallas_call x0 -> x9, Pallas kernels: none -> 35 us  [the longest x1 22.4 us: refresh(): pl.pallas_call(refresh_kernel, out_shape=(jax.ShapeDtypeStruct((2, width,...]
    all_gather x1 -> x0, waiting for transfers between devices: 23.9 us -> none  [body(): back = lax.all_gather(mine, 'dp', axis=0, tiled=True)]
    ppermute x0 -> x6, starting transfers between devices: none -> 8.11 us  [shift(): lax.ppermute(value, 'dp', [(i, (i + by) % n_data) for i in range(n_data)])]
    unnamed x14, local copies, waits for them, and re-layouts: 1.76 us -> 8.18 us
    ppermute x0 -> x6, waiting for transfers between devices: none -> 5.29 us  [shift(): lax.ppermute(value, 'dp', [(i, (i + by) % n_data) for i in range(n_data)])]
    gather x2 -> x1, local copies, waits for them, and re-layouts: 5.73 us -> 2.07 us  [body(): local.at[order]]
    broadcast_in_dim x1 -> x0, other arithmetic: 2.72 us -> none  [body(): new_roots = jnp.stack([root_left, root_right], axis=0)[None]]
  transfers between devices with their start and end apart: 2 -> 7, of which waited for: 2 -> 3; matrix products, arithmetic and copies ran while one was open for 6% -> 0% of each run, Pallas kernels for 0% -> 8%
where the time goes in v2:
time: 146 us; the launch traced here: 145 us
  waiting for transfers between devices  50.1 us (34%)
  Pallas kernels  35 us (24%)
  starting transfers between devices  24.8 us (17%)
  blocking collectives  23.2 us (16%)
  local copies, waits for them, and re-layouts  10.3 us (7%)
    all_to_all x1, waiting for transfers between devices, body(): lax.all_to_all(outgoing, ('dp', 'fsdp'), split_axis=0, concat_axis=0, til...  44.8 us
    all_to_all x1, blocking collectives, body(): lax.all_to_all(pieces, 'fsdp', split_axis=0, concat_axis=0, tiled=True)  23.2 us
    pallas_call x1, Pallas kernels, refresh(): pl.pallas_call(refresh_kernel, out_shape=(jax.ShapeDtypeStruct((2, width,...  22.4 us
    all_to_all x1, starting transfers between devices, body(): lax.all_to_all(outgoing, ('dp', 'fsdp'), split_axis=0, concat_axis=0, til...  16.7 us
    pallas_call x7, Pallas kernels, place(): pl.pallas_call(functools.partial(place_kernel, owners, offset), out_shape...  9.14 us
    unnamed x14, local copies, waits for them, and re-layouts  8.18 us
    ppermute x6, starting transfers between devices, shift(): lax.ppermute(value, 'dp', [(i, (i + by) % n_data) for i in range(n_data)])  8.11 us
    ppermute x6, waiting for transfers between devices, shift(): lax.ppermute(value, 'dp', [(i, (i + by) % n_data) for i in range(n_data)])  5.29 us
  transfers between devices with their start and end apart: 7, of which 3 were waited for; matrix products, arithmetic and copies ran while one was open for 0% of the time, Pallas kernels for 8%

profile of v2, /device:TPU:1, one launch (start us, length us, event | category | flops | bytes accessed | tf_op | source)
XLA Modules:
  0.0 145.2 jit_solution(4640660009155233085)
XLA Ops:
  0.6 0.0 copy-start
  0.6 0.8 pad_clamp_fusion
  1.5 0.8 copy-done
  2.2 2.1 %gather_fusion = bf16[256,8,512]{2,1,0:T(8,128)(2,1)} fusion(bf16[256,8,512]{2,1,0:T(8,128)(2,1)S(1)} %bitcast.5, s32[1024]{0:T(1024)S(1)} %pad_clamp_fusion), kind=kCustom, calls=%fused_computation | custom fusion | bytes 4195328 | tf_op jit(solution)/shard_map/gather | solution.py:218
  4.3 16.7 %all-to-all-start = ((bf16[256,8,512]{2,1,0:T(8,128)(2,1)}), bf16[256,8,512]{2,1,0:T(8,128)(2,1)}, u32[]{:S(2)}, u32[]{:S(2)}) async-start(bf16[256,8,512]{2,1,0:T(8,128)(2,1)} %gather_fusion), calls=%async_computation | async-start | bytes 4194304 | tf_op jit(solution)/shard_map/all_to_all | solution.py:221
  21.0 0.0 copy-start.2
  21.0 1.6 %copy-done.2 = f32[1,2,512,512]{3,2,1,0:T(8,128)S(1)} copy-done((f32[1,2,512,512]{3,2,1,0:T(8,128)S(1)}, f32[1,2,512,512]{3,2,1,0:T(8,128)}, u32[]{:S(2)}) %copy-start.2) | copy-done | bytes 2097176
  22.6 3.4 %fourth_powers.1 = (bf16[2,2,512,512]{3,2,1,0:T(8,128)(2,1)S(1)}, bf16[2,2,512,512]{3,2,1,0:T(8,128)(2,1)S(1)}) custom-call(f32[2,512,512]{2,1,0:T(8,128)S(1)} %bitcast.7), custom_call_target="tpu_custom_call" | custom-call | flops 3221225472 | bytes 6291456 | tf_op jit(solution)/shard_map/fourth_powers/pallas_call | solution.py:56
  26.0 0.0 copy-start.3
  26.0 1.3 copy-done.3
  27.3 0.0 copy-start.5
  27.3 1.3 copy-done.5
  28.7 44.8 %all-to-all-done = bf16[256,8,512]{2,1,0:T(8,128)(2,1)} async-done(((bf16[256,8,512]{2,1,0:T(8,128)(2,1)}), bf16[256,8,512]{2,1,0:T(8,128)(2,1)}, u32[]{:S(2)}, u32[]{:S(2)}) %all-to-all-start) | async-done | bytes 2097184 | tf_op jit(solution)/shard_map/all_to_all | solution.py:221
  73.5 0.0 copy-start.4
  73.5 1.6 %copy-done.4 = bf16[2,2,512,512]{3,2,1,0:T(8,128)(2,1)S(1)} copy-done((bf16[2,2,512,512]{3,2,1,0:T(8,128)(2,1)S(1)}, bf16[2,2,512,512]{3,2,1,0:T(8,128)(2,1)}, u32[]{:S(2)}) %copy-start.4) | copy-done | bytes 2097176
  75.1 0.0 copy-start.6
  75.1 1.6 %copy-done.6 = bf16[2,2,512,512]{3,2,1,0:T(8,128)(2,1)S(1)} copy-done((bf16[2,2,512,512]{3,2,1,0:T(8,128)(2,1)S(1)}, bf16[2,2,512,512]{3,2,1,0:T(8,128)(2,1)}, u32[]{:S(2)}) %copy-start.6) | copy-done | bytes 2097176
  76.7 22.4 %refresh_roots.1 = (f32[2,512,512]{2,1,0:T(8,128)}, bf16[512,512]{1,0:T(8,128)(2,1)S(1)}) custom-call(bf16[4,512,512]{2,1,0:T(8,128)(2,1)} %bitcast.1.arrived, bf16[2,2,512,512]{3,2,1,0:T(8,128)(2,1)S(1)} %copy-done.4, bf16[2,2,512,512]{3,2,1,0:T(8,128)(2,1)S(1)} %copy-done.6), custom_call_target="tpu_custom_call" | custom-call | flops 19864223744 | bytes 9437184 | tf_op jit(solution)/shard_map/refresh_roots/pallas_call | solution.py:154
  99.1 0.0 copy-start.1
  99.1 23.2 %all_to_all.10.source = bf16[64,8,512]{2,1,0:T(8,128)(2,1)S(1)} all-to-all(bf16[64,8,512]{2,1,0:T(8,128)(2,1)S(1)} %bitcast.6), channel_id=1, replica_groups=mesh['dp'=4,'fsdp'=64] {'fsdp'}, dimensions={0} | all-to-all | bytes 1048576 | tf_op jit(solution)/shard_map/all_to_all | solution.py:225
  122.4 0.4 collective-permute-start.2
  122.8 2.4 %collective-permute-start = (bf16[32,8,512]{2,1,0:T(8,128)(2,1)S(1)}, bf16[32,8,512]{2,1,0:T(8,128)(2,1)S(1)}, u32[]{:S(2)}, u32[]{:S(2)}) collective-permute-start(bf16[32,8,512]{2,1,0:T(8,128)(2,1)S(1)} %get-tuple-element.11), channel_id=1, source_target_pairs={{0,192},{64,0},{128,64},{192,128},{1,193},{65,1},{129,65},{193,129... | collective-permute-start | bytes 786440 | tf_op jit(solution)/shard_map/ppermute | solution.py:230
  125.2 0.0 collective-permute-start.5
  125.2 2.7 %collective-permute-start.4 = (bf16[32,8,512]{2,1,0:T(8,128)(2,1)S(1)}, bf16[32,8,512]{2,1,0:T(8,128)(2,1)S(1)}, u32[]{:S(2)}, u32[]{:S(2)}) collective-permute-start(bf16[32,8,512]{2,1,0:T(8,128)(2,1)S(1)} %get-tuple-element.10), channel_id=1, source_target_pairs={{0,192},{64,0},{128,64},{192,128},{1,193},{65,1},{129,65},{193,129... | collective-permute-start | bytes 786440 | tf_op jit(solution)/shard_map/ppermute | solution.py:230
  127.8 3.3 %collective-permute-done.2.source = bf16[32,8,512]{2,1,0:T(8,128)(2,1)S(1)} collective-permute-done((bf16[32,8,512]{2,1,0:T(8,128)(2,1)S(1)}, bf16[32,8,512]{2,1,0:T(8,128)(2,1)S(1)}, u32[]{:S(2)}, u32[]{:S(2)}) %collective-permute-start.2) | collective-permute-done | bytes 262176 | tf_op jit(solution)/shard_map/ppermute | solution.py:230
  131.2 0.0 collective-permute-start.3
  131.2 0.0 collective-permute-done.source
  131.2 2.7 %collective-permute-start.1 = (bf16[32,8,512]{2,1,0:T(8,128)(2,1)S(1)}, bf16[32,8,512]{2,1,0:T(8,128)(2,1)S(1)}, u32[]{:S(2)}, u32[]{:S(2)}) collective-permute-start(bf16[32,8,512]{2,1,0:T(8,128)(2,1)S(1)} %collective-permute-done.source), channel_id=1, source_target_pairs={{0,192},{64,0},{128,64},{192,128},{1,193},{65,1},{129,65},{193,129... | collective-permute-start | bytes 786440 | tf_op jit(solution)/shard_map/ppermute | solution.py:230
  133.9 0.0 copy-done.1
  133.9 1.4 place_blocks.7.rest_0_
  135.3 1.3 place_blocks.8.rest_0_
  136.6 1.3 place_blocks.9.rest_0_
  137.9 0.0 collective-permute-done.5.source
  137.9 1.3 place_blocks.10.rest_0_
  139.2 0.0 collective-permute-done.4.source
  139.2 1.3 place_blocks.11.rest_0_
  140.5 1.9 %collective-permute-done.3.source = bf16[32,8,512]{2,1,0:T(8,128)(2,1)S(1)} collective-permute-done((bf16[32,8,512]{2,1,0:T(8,128)(2,1)S(1)}, bf16[32,8,512]{2,1,0:T(8,128)(2,1)S(1)}, u32[]{:S(2)}, u32[]{:S(2)}) %collective-permute-start.3) | collective-permute-done | bytes 262176 | tf_op jit(solution)/shard_map/ppermute | solution.py:230
  142.4 1.3 place_blocks.12.rest_0_
  143.7 0.0 collective-permute-done.1.source
  143.7 1.3 place_blocks.13
  (1 shorter events, 0.0 us)
Async XLA Ops:
  0.6 1.6 %copy-start = (bf16[1,256,8,512]{3,2,1,0:T(8,128)(2,1)S(1)}, bf16[1,256,8,512]{3,2,1,0:T(8,128)(2,1)}, u32[]{:S(2)}) copy-start(bf16[1,256,8,512]{3,2,1,0:T(8,128)(2,1)} %param.3) | copy-start | bytes 6291460
  4.3 69.2 %all-to-all-start = ((bf16[256,8,512]{2,1,0:T(8,128)(2,1)}), bf16[256,8,512]{2,1,0:T(8,128)(2,1)}, u32[]{:S(2)}, u32[]{:S(2)}) async-start(bf16[256,8,512]{2,1,0:T(8,128)(2,1)} %gather_fusion), calls=%async_computation | async-start | bytes 4194304 | tf_op jit(solution)/shard_map/all_to_all | solution.py:221
  21.0 1.6 %copy-start.2 = (f32[1,2,512,512]{3,2,1,0:T(8,128)S(1)}, f32[1,2,512,512]{3,2,1,0:T(8,128)}, u32[]{:S(2)}) copy-start(f32[1,2,512,512]{3,2,1,0:T(8,128)} %param.5) | copy-start | bytes 6291460
  26.0 1.3 copy-start.3
  27.3 1.3 copy-start.5
  73.5 1.6 %copy-start.4 = (bf16[2,2,512,512]{3,2,1,0:T(8,128)(2,1)S(1)}, bf16[2,2,512,512]{3,2,1,0:T(8,128)(2,1)}, u32[]{:S(2)}) copy-start(bf16[2,2,512,512]{3,2,1,0:T(8,128)(2,1)} %copy-done.3) | copy-start | bytes 6291460
  75.1 1.6 %copy-start.6 = (bf16[2,2,512,512]{3,2,1,0:T(8,128)(2,1)S(1)}, bf16[2,2,512,512]{3,2,1,0:T(8,128)(2,1)}, u32[]{:S(2)}) copy-start(bf16[2,2,512,512]{3,2,1,0:T(8,128)(2,1)} %copy-done.5) | copy-start | bytes 6291460
  99.1 34.8 %copy-start.1 = (s32[256]{0:T(256)S(1)}, s32[256]{0:T(256)}, u32[]{:S(2)}) copy-start(s32[256]{0:T(256)} %order.13) | copy-start | bytes 3076
  122.4 8.8 %collective-permute-start.2 = (bf16[32,8,512]{2,1,0:T(8,128)(2,1)S(1)}, bf16[32,8,512]{2,1,0:T(8,128)(2,1)S(1)}, u32[]{:S(2)}, u32[]{:S(2)}) collective-permute-start(bf16[32,8,512]{2,1,0:T(8,128)(2,1)S(1)} %get-tuple-element.10), channel_id=1, source_target_pairs={{0,64},{64,128},{128,192},{192,0},{1,65},{65,129},{129,193},{193,1... | collective-permute-start | bytes 786440 | tf_op jit(solution)/shard_map/ppermute | solution.py:230
  122.8 8.4 %collective-permute-start = (bf16[32,8,512]{2,1,0:T(8,128)(2,1)S(1)}, bf16[32,8,512]{2,1,0:T(8,128)(2,1)S(1)}, u32[]{:S(2)}, u32[]{:S(2)}) collective-permute-start(bf16[32,8,512]{2,1,0:T(8,128)(2,1)S(1)} %get-tuple-element.11), channel_id=1, source_target_pairs={{0,192},{64,0},{128,64},{192,128},{1,193},{65,1},{129,65},{193,129... | collective-permute-start | bytes 786440 | tf_op jit(solution)/shard_map/ppermute | solution.py:230
  125.2 12.7 %collective-permute-start.5 = (bf16[32,8,512]{2,1,0:T(8,128)(2,1)S(1)}, bf16[32,8,512]{2,1,0:T(8,128)(2,1)S(1)}, u32[]{:S(2)}, u32[]{:S(2)}) collective-permute-start(bf16[32,8,512]{2,1,0:T(8,128)(2,1)S(1)} %get-tuple-element.11), channel_id=1, source_target_pairs={{0,64},{64,128},{128,192},{192,0},{1,65},{65,129},{129,193},{193,1... | collective-permute-start | bytes 786440 | tf_op jit(solution)/shard_map/ppermute | solution.py:230
  125.2 14.0 %collective-permute-start.4 = (bf16[32,8,512]{2,1,0:T(8,128)(2,1)S(1)}, bf16[32,8,512]{2,1,0:T(8,128)(2,1)S(1)}, u32[]{:S(2)}, u32[]{:S(2)}) collective-permute-start(bf16[32,8,512]{2,1,0:T(8,128)(2,1)S(1)} %get-tuple-element.10), channel_id=1, source_target_pairs={{0,192},{64,0},{128,64},{192,128},{1,193},{65,1},{129,65},{193,129... | collective-permute-start | bytes 786440 | tf_op jit(solution)/shard_map/ppermute | solution.py:230
  131.2 11.2 %collective-permute-start.3 = (bf16[32,8,512]{2,1,0:T(8,128)(2,1)S(1)}, bf16[32,8,512]{2,1,0:T(8,128)(2,1)S(1)}, u32[]{:S(2)}, u32[]{:S(2)}) collective-permute-start(bf16[32,8,512]{2,1,0:T(8,128)(2,1)S(1)} %collective-permute-done.2.source), channel_id=1, source_target_pairs={{0,64},{64,128},{128,192},{192,0},{1,65},{65,129},{129,193},{193,1... | collective-permute-start | bytes 786440 | tf_op jit(solution)/shard_map/ppermute | solution.py:230
  131.2 12.5 %collective-permute-start.1 = (bf16[32,8,512]{2,1,0:T(8,128)(2,1)S(1)}, bf16[32,8,512]{2,1,0:T(8,128)(2,1)S(1)}, u32[]{:S(2)}, u32[]{:S(2)}) collective-permute-start(bf16[32,8,512]{2,1,0:T(8,128)(2,1)S(1)} %collective-permute-done.source), channel_id=1, source_target_pairs={{0,192},{64,0},{128,64},{192,128},{1,193},{65,1},{129,65},{193,129... | collective-permute-start | bytes 786440 | tf_op jit(solution)/shard_map/ppermute | solution.py:230

commit v3 on v2

v3 whole, which is shorter than its diff:
```python
import functools

import jax
import jax.numpy as jnp
from jax import lax
from jax.experimental import pallas as pl
from jax.experimental.pallas import tpu as pltpu
from jax.sharding import PartitionSpec as P

ITERS = 3
MB = 1 << 20
BF16 = jnp.bfloat16
F32 = jnp.float32
ANY = pl.BlockSpec(memory_space=pl.ANY)
VMEM = pl.BlockSpec(memory_space=pltpu.VMEM)
SMEM = pl.BlockSpec(memory_space=pltpu.SMEM)


def split(value):
    high = value.astype(BF16)
    return high, (value - high.astype(F32)).astype(BF16)


def product3(lhs, rhs, rows):
    high = lhs[0, rows, :]
    left = jnp.concatenate([high, lhs[1, rows, :], high], axis=1)
    over = rhs[0]
    right = jnp.concatenate([over, over, rhs[1]], axis=0)
    return jnp.dot(left, right, preferred_element_type=F32)


def keep(target, rows, value):
    high, low = split(value)
    target[0, rows, :] = high
    target[1, rows, :] = low


def halves(width):
    size = width // 2
    return [pl.ds(0, size), pl.ds(size, size)]


def fourth_kernel(prev, x_out, q_out, square):
    width = prev.shape[-1]
    for side in range(2):
        keep(x_out.at[side], slice(None), prev[side])
    for source, target in ((x_out, square), (square, q_out)):
        for rows in halves(width):
            for side in range(2):
                keep(target.at[side], rows, product3(source.at[side], source.at[side], rows))


def fourth_powers(prev):
    width = prev.shape[-1]
    pair = jax.ShapeDtypeStruct((2, 2, width, width), BF16)
    return pl.pallas_call(
        fourth_kernel,
        out_shape=(pair, pair),
        in_specs=[VMEM],
        out_specs=(VMEM, VMEM),
        scratch_shapes=[pltpu.VMEM((2, 2, width, width), BF16)],
        compiler_params=pltpu.CompilerParams(vmem_limit_bytes=20 * MB),
        cost_estimate=pl.CostEstimate(
            flops=2 * 2 * 3 * 2 * width**3, bytes_accessed=6 * MB, transcendentals=0
        ),
        name="fourth_powers",
    )(prev)


def refresh_kernel(
    arrived, x, q, roots, out,
    grads, partial, stat, moment, factor, power, root, final, mean, mixed, sems,
):
    n_micro, width = grads.shape[0], grads.shape[-1]
    parts = halves(width)
    size = width // 2
    batches = [pl.ds(0, n_micro // 2), pl.ds(n_micro // 2, n_micro // 2)]
    copies = [
        pltpu.make_async_copy(arrived.at[batch], grads.at[batch], sems.at[number])
        for number, batch in enumerate(batches)
    ]
    for copy in copies:
        copy.start()
    contracts = ((((1,), (1,)), ((), ())), (((0,), (0,)), ((), ())))
    totals = [jnp.zeros((1, 1), F32), jnp.zeros((1, 1), F32)]
    for number, copy in enumerate(copies):
        copy.wait()
        first = number * (n_micro // 2)
        whole = [grads[d] for d in range(first, first + n_micro // 2)]
        for side in range(2):
            rhs = jnp.concatenate(whole, axis=1 - side)
            for index, rows in enumerate(parts):
                lo, hi = index * size, (index + 1) * size
                lhs = rhs[lo:hi, :] if side == 0 else rhs[:, lo:hi]
                value = lax.dot_general(lhs, rhs, contracts[side], preferred_element_type=F32)
                if number == 0:
                    partial[side, rows, :] = value
                else:
                    value = value + partial[side, rows, :]
                    totals[side] = totals[side] + jnp.sum(
                        value * value, axis=(0, 1), keepdims=True
                    )
                    keep(stat.at[side], rows, value)
    scales = [1.0 / (jnp.sqrt(total / (width * width) + 1e-06) * width) for total in totals]

    row_ids = lax.broadcasted_iota(jnp.int32, (size, width), 0)
    col_ids = lax.broadcasted_iota(jnp.int32, (size, width), 1)

    def keep_factor(side, index, rows, value):
        diagonal = jnp.where(row_ids + index * size == col_ids, 1.25, 0.0)
        keep(factor.at[side], rows, diagonal - 0.25 * value)

    for side in range(2):
        for index, rows in enumerate(parts):
            value = product3(q.at[side], stat.at[side], rows) * scales[side]
            keep(moment.at[0, side], rows, value)
            keep_factor(side, index, rows, value)
    for index, rows in enumerate(parts):
        value = grads[0, rows, :].astype(F32)
        for d in range(1, n_micro):
            value = value + grads[d, rows, :].astype(F32)
        keep(mean, rows, value / n_micro)
    held = x
    for step in range(ITERS - 1):
        for side in range(2):
            for rows in parts:
                keep(
                    power.at[0, side], rows, product3(factor.at[side], factor.at[side], rows)
                )
        for side in range(2):
            for rows in parts:
                keep(
                    power.at[1, side],
                    rows,
                    product3(power.at[0, side], power.at[0, side], rows),
                )
        for side in range(2):
            for rows in parts:
                keep(
                    root.at[step % 2, side], rows, product3(held.at[side], factor.at[side], rows)
                )
        held = root.at[step % 2]
        for side in range(2):
            for index, rows in enumerate(parts):
                value = product3(power.at[1, side], moment.at[step % 2, side], rows)
                if step + 2 < ITERS:
                    keep(moment.at[(step + 1) % 2, side], rows, value)
                keep_factor(side, index, rows, value)
    last = root.at[(ITERS - 1) % 2]
    writes = []
    for side in range(2):
        for rows in parts:
            value = product3(held.at[side], factor.at[side], rows)
            final[side, rows, :] = value
            keep(last.at[side], rows, value)
        write = pltpu.make_async_copy(final.at[side], roots.at[side], sems.at[side])
        write.start()
        writes.append(write)
    for rows in parts:
        keep(mixed, rows, product3(last.at[0], mean, rows))
    for rows in parts:
        out[rows, :] = product3(mixed, last.at[1], rows).astype(BF16)
    for write in writes:
        write.wait()


def refresh(arrived, x, q):
    n_micro, width = arrived.shape[0], arrived.shape[-1]
    matrix = (2, 2, width, width)
    return pl.pallas_call(
        refresh_kernel,
        out_shape=(
            jax.ShapeDtypeStruct((2, width, width), F32),
            jax.ShapeDtypeStruct((width, width), BF16),
        ),
        in_specs=[ANY, VMEM, VMEM],
        out_specs=(ANY, VMEM),
        scratch_shapes=[
            pltpu.VMEM((n_micro, width, width), BF16),
            pltpu.VMEM((2, width, width), F32),
            pltpu.VMEM(matrix, BF16),
            pltpu.VMEM((2,) + matrix, BF16),
            pltpu.VMEM(matrix, BF16),
            pltpu.VMEM((2,) + matrix, BF16),
            pltpu.VMEM((2,) + matrix, BF16),
            pltpu.VMEM((2, width, width), F32),
            pltpu.VMEM((2, width, width), BF16),
            pltpu.VMEM((2, width, width), BF16),
            pltpu.SemaphoreType.DMA((2,)),
        ],
        compiler_params=pltpu.CompilerParams(vmem_limit_bytes=30 * MB),
        cost_estimate=pl.CostEstimate(
            flops=(22 * 3 + 8) * 2 * width**3, bytes_accessed=9 * MB, transcendentals=0
        ),
        name="refresh_roots",
    )(arrived, x, q)


def place_kernel(owners, offsets, order, *refs):
    pieces, (out, sems) = refs[: len(offsets)], refs[-2:]
    n_data, mine = lax.axis_size("dp"), lax.axis_index("dp")
    for number, (piece, (by, skip)) in enumerate(zip(pieces, offsets)):
        base = lax.rem(mine + by, n_data) * owners + skip
        for i in range(piece.shape[0]):
            pltpu.make_async_copy(
                piece.at[i], out.at[order[base + i]], sems.at[number]
            ).start()
    for number, piece in enumerate(pieces):
        pltpu.make_async_copy(piece, out.at[pl.ds(0, piece.shape[0])], sems.at[number]).wait()


def place(owners, order, batch, base):
    offsets, pieces = zip(*batch)
    rows, width = pieces[0].shape[1:]
    count = len(pieces)
    args, specs, aliases = [order, *pieces], [SMEM] + [VMEM] * count, {}
    if base is not None:
        args.append(base)
        specs.append(ANY)
        aliases = {count + 1: 0}
    return pl.pallas_call(
        functools.partial(place_kernel, owners, offsets),
        out_shape=jax.ShapeDtypeStruct((order.shape[0], rows, width), BF16),
        in_specs=specs,
        out_specs=ANY,
        scratch_shapes=[pltpu.SemaphoreType.DMA((count,))],
        input_output_aliases=aliases,
        compiler_params=pltpu.CompilerParams(vmem_limit_bytes=8 * MB),
        cost_estimate=pl.CostEstimate(
            flops=0, bytes_accessed=4 * sum(p.size for p in pieces), transcendentals=0
        ),
        name="place_blocks",
    )(*args)


def body(grads, order, prev_roots):
    n_data = lax.axis_size("dp")
    local = grads[0]
    rows, width = local.shape[1:]
    outgoing = local.at[order].get(
        mode="promise_in_bounds", unique_indices=True, wrap_negative_indices=False
    )
    arrived = lax.all_to_all(outgoing, ("dp", "fsdp"), split_axis=0, concat_axis=0, tiled=True)
    x, q = fourth_powers(prev_roots[0])
    roots, refreshed = refresh(arrived.reshape(n_data, width, width), x, q)
    pieces = refreshed.reshape(width // rows, rows, width)
    mine = lax.all_to_all(pieces, "fsdp", split_axis=0, concat_axis=0, tiled=True)
    owners = mine.shape[0]
    half = owners // 2

    def shift(value, by):
        return lax.ppermute(value, "dp", [(i, (i + by) % n_data) for i in range(n_data)])

    low, high = mine[:half], mine[half:]
    low_up, high_down = shift(low, 1), shift(high, -1)
    high_up, low_down = shift(high, 1), shift(low, -1)
    low_far, high_far = shift(low_up, 1), shift(high_down, -1)
    result = None
    for batch in (
        (((0, 0), mine), ((n_data - 1, 0), low_up), ((1, half), high_down)),
        (((n_data - 1, half), high_up), ((1, 0), low_down)),
        (((n_data - 2, 0), low_far), ((2, half), high_far)),
    ):
        result = place(owners, order, batch, result)
    return (result, roots[None])


def solution(mesh):
    return jax.shard_map(
        body,
        mesh=mesh,
        in_specs=(P("dp", None, "fsdp", None), P(), P(("dp", "fsdp"), None, None, None)),
        out_specs=(P(None, "fsdp", None), P(("dp", "fsdp"), None, None, None)),
        check_vma=False,
    )
```

time: 146 us -> 145 us (level)
  waiting for transfers between devices: 50.1 us -> 56 us
  Pallas kernels: 35 us -> 30.1 us
  starting transfers between devices: 24.8 us -> 23 us
    ppermute x6, waiting for transfers between devices: 5.29 us -> 11.2 us  [shift(): lax.ppermute(value, 'dp', [(i, (i + by) % n_data) for i in range(n_data)])]
    pallas_call x7 -> x3, Pallas kernels: 9.14 us -> 4.48 us  [place(): pl.pallas_call(functools.partial(place_kernel, owners, offsets), out_shap...]
    ppermute x6, starting transfers between devices: 8.11 us -> 6.32 us  [shift(): lax.ppermute(value, 'dp', [(i, (i + by) % n_data) for i in range(n_data)])]
  transfers between devices with their start and end apart: 7 -> 7, of which waited for: 3 -> 5; matrix products, arithmetic and copies ran while one was open for 0% -> 0% of each run, Pallas kernels for 8% -> 5%
where the time goes in v3:
time: 145 us; the launch traced here: 144 us
  waiting for transfers between devices  56 us (39%)
  Pallas kernels  30.1 us (21%)
  blocking collectives  23.2 us (16%)
  starting transfers between devices  23 us (16%)
  local copies, waits for them, and re-layouts  10.3 us (7%)
    all_to_all x1, waiting for transfers between devices, body(): lax.all_to_all(outgoing, ('dp', 'fsdp'), split_axis=0, concat_axis=0, til...  44.8 us
    all_to_all x1, blocking collectives, body(): lax.all_to_all(pieces, 'fsdp', split_axis=0, concat_axis=0, tiled=True)  23.2 us
    pallas_call x1, Pallas kernels, refresh(): pl.pallas_call(refresh_kernel, out_shape=(jax.ShapeDtypeStruct((2, width,...  22.2 us
    all_to_all x1, starting transfers between devices, body(): lax.all_to_all(outgoing, ('dp', 'fsdp'), split_axis=0, concat_axis=0, til...  16.7 us
    ppermute x6, waiting for transfers between devices, shift(): lax.ppermute(value, 'dp', [(i, (i + by) % n_data) for i in range(n_data)])  11.2 us
    unnamed x14, local copies, waits for them, and re-layouts  8.18 us
    ppermute x6, starting transfers between devices, shift(): lax.ppermute(value, 'dp', [(i, (i + by) % n_data) for i in range(n_data)])  6.32 us
    pallas_call x3, Pallas kernels, place(): pl.pallas_call(functools.partial(place_kernel, owners, offsets), out_shap...  4.48 us
  transfers between devices with their start and end apart: 7, of which 5 were waited for; matrix products, arithmetic and copies ran while one was open for 0% of the time, Pallas kernels for 5%

profile of v3, /device:TPU:1, one launch (start us, length us, event | category | flops | bytes accessed | tf_op | source)
XLA Modules:
  0.0 144.3 jit_solution(14616247733480959405)
XLA Ops:
  0.6 0.0 copy-start
  0.6 0.8 pad_clamp_fusion
  1.5 0.8 copy-done
  2.2 2.1 %gather_fusion = bf16[256,8,512]{2,1,0:T(8,128)(2,1)} fusion(bf16[256,8,512]{2,1,0:T(8,128)(2,1)S(1)} %bitcast.5, s32[1024]{0:T(1024)S(1)} %pad_clamp_fusion), kind=kCustom, calls=%fused_computation | custom fusion | bytes 4195328 | tf_op jit(solution)/shard_map/gather | solution.py:240
  4.3 16.7 %all-to-all-start = ((bf16[256,8,512]{2,1,0:T(8,128)(2,1)}), bf16[256,8,512]{2,1,0:T(8,128)(2,1)}, u32[]{:S(2)}, u32[]{:S(2)}) async-start(bf16[256,8,512]{2,1,0:T(8,128)(2,1)} %gather_fusion), calls=%async_computation | async-start | bytes 4194304 | tf_op jit(solution)/shard_map/all_to_all | solution.py:243
  21.0 0.0 copy-start.2
  21.0 1.6 %copy-done.2 = f32[1,2,512,512]{3,2,1,0:T(8,128)S(1)} copy-done((f32[1,2,512,512]{3,2,1,0:T(8,128)S(1)}, f32[1,2,512,512]{3,2,1,0:T(8,128)}, u32[]{:S(2)}) %copy-start.2) | copy-done | bytes 2097176
  22.6 3.4 %fourth_powers.1 = (bf16[2,2,512,512]{3,2,1,0:T(8,128)(2,1)S(1)}, bf16[2,2,512,512]{3,2,1,0:T(8,128)(2,1)S(1)}) custom-call(f32[2,512,512]{2,1,0:T(8,128)S(1)} %bitcast.7), custom_call_target="tpu_custom_call" | custom-call | flops 3221225472 | bytes 6291456 | tf_op jit(solution)/shard_map/fourth_powers/pallas_call | solution.py:56
  26.0 0.0 copy-start.3
  26.0 1.3 copy-done.3
  27.3 0.0 copy-start.5
  27.3 1.3 copy-done.5
  28.7 44.8 %all-to-all-done = bf16[256,8,512]{2,1,0:T(8,128)(2,1)} async-done(((bf16[256,8,512]{2,1,0:T(8,128)(2,1)}), bf16[256,8,512]{2,1,0:T(8,128)(2,1)}, u32[]{:S(2)}, u32[]{:S(2)}) %all-to-all-start) | async-done | bytes 2097184 | tf_op jit(solution)/shard_map/all_to_all | solution.py:243
  73.5 0.0 copy-start.4
  73.5 1.6 %copy-done.4 = bf16[2,2,512,512]{3,2,1,0:T(8,128)(2,1)S(1)} copy-done((bf16[2,2,512,512]{3,2,1,0:T(8,128)(2,1)S(1)}, bf16[2,2,512,512]{3,2,1,0:T(8,128)(2,1)}, u32[]{:S(2)}) %copy-start.4) | copy-done | bytes 2097176
  75.1 0.0 copy-start.6
  75.1 1.6 %copy-done.6 = bf16[2,2,512,512]{3,2,1,0:T(8,128)(2,1)S(1)} copy-done((bf16[2,2,512,512]{3,2,1,0:T(8,128)(2,1)S(1)}, bf16[2,2,512,512]{3,2,1,0:T(8,128)(2,1)}, u32[]{:S(2)}) %copy-start.6) | copy-done | bytes 2097176
  76.7 22.2 %refresh_roots.1 = (f32[2,512,512]{2,1,0:T(8,128)}, bf16[512,512]{1,0:T(8,128)(2,1)S(1)}) custom-call(bf16[4,512,512]{2,1,0:T(8,128)(2,1)} %bitcast.1.arrived, bf16[2,2,512,512]{3,2,1,0:T(8,128)(2,1)S(1)} %copy-done.4, bf16[2,2,512,512]{3,2,1,0:T(8,128)(2,1)S(1)} %copy-done.6), custom_call_target="tpu_custom_call" | custom-call | flops 19864223744 | bytes 9437184 | tf_op jit(solution)/shard_map/refresh_roots/pallas_call | solution.py:170
  98.8 0.0 copy-start.1
  98.8 23.2 %all_to_all.10.refs_0_ = bf16[64,8,512]{2,1,0:T(8,128)(2,1)S(1)} all-to-all(bf16[64,8,512]{2,1,0:T(8,128)(2,1)S(1)} %bitcast.6), channel_id=1, replica_groups=mesh['dp'=4,'fsdp'=64] {'fsdp'}, dimensions={0} | all-to-all | bytes 1048576 | tf_op jit(solution)/shard_map/all_to_all | solution.py:247
  122.1 0.9 collective-permute-start.2
  123.1 0.6 collective-permute-start
  123.7 0.3 collective-permute-start.4
  124.0 2.4 %collective-permute-start.5 = (bf16[32,8,512]{2,1,0:T(8,128)(2,1)S(1)}, bf16[32,8,512]{2,1,0:T(8,128)(2,1)S(1)}, u32[]{:S(2)}, u32[]{:S(2)}) collective-permute-start(bf16[32,8,512]{2,1,0:T(8,128)(2,1)S(1)} %get-tuple-element.11), channel_id=1, source_target_pairs={{0,192},{64,0},{128,64},{192,128},{1,193},{65,1},{129,65},{193,129... | collective-permute-start | bytes 786440 | tf_op jit(solution)/shard_map/ppermute | solution.py:252
  126.4 3.3 %collective-permute-done.2.refs_2_ = bf16[32,8,512]{2,1,0:T(8,128)(2,1)S(1)} collective-permute-done((bf16[32,8,512]{2,1,0:T(8,128)(2,1)S(1)}, bf16[32,8,512]{2,1,0:T(8,128)(2,1)S(1)}, u32[]{:S(2)}, u32[]{:S(2)}) %collective-permute-start.2) | collective-permute-done | bytes 262176 | tf_op jit(solution)/shard_map/ppermute | solution.py:252
  129.7 2.1 %collective-permute-start.3 = (bf16[32,8,512]{2,1,0:T(8,128)(2,1)S(1)}, bf16[32,8,512]{2,1,0:T(8,128)(2,1)S(1)}, u32[]{:S(2)}, u32[]{:S(2)}) collective-permute-start(bf16[32,8,512]{2,1,0:T(8,128)(2,1)S(1)} %collective-permute-done.2.refs_2_), channel_id=1, source_target_pairs={{0,192},{64,0},{128,64},{192,128},{1,193},{65,1},{129,65},{193,129... | collective-permute-start | bytes 786440 | tf_op jit(solution)/shard_map/ppermute | solution.py:252
  131.8 0.0 collective-permute-done.refs_1_
  131.8 0.0 collective-permute-start.1
  131.8 0.0 copy-done.1
  131.8 1.7 %place_blocks.3.refs_2_ = bf16[256,8,512]{2,1,0:T(8,128)(2,1)} custom-call(s32[256]{0:T(256)S(1)} %copy-done.1, bf16[64,8,512]{2,1,0:T(8,128)(2,1)S(1)} %all_to_all.10.refs_0_, bf16[32,8,512]{2,1,0:T(8,128)(2,1)S(1)} %collective-permute-done.refs_1_, bf16[32,8,512]{2,1,0:T(8,128)(2,1)S(1)} %collective-permute-done.2.refs_2_), custom_call_target="tpu_custom_call" | custom-call | bytes 2097152 | tf_op jit(solution)/shard_map/place_blocks/pallas_call | solution.py:221
  133.5 3.6 %collective-permute-done.4.refs_0_ = bf16[32,8,512]{2,1,0:T(8,128)(2,1)S(1)} collective-permute-done((bf16[32,8,512]{2,1,0:T(8,128)(2,1)S(1)}, bf16[32,8,512]{2,1,0:T(8,128)(2,1)S(1)}, u32[]{:S(2)}, u32[]{:S(2)}) %collective-permute-start.4) | collective-permute-done | bytes 262176 | tf_op jit(solution)/shard_map/ppermute | solution.py:252
  137.1 0.0 collective-permute-done.5.refs_1_
  137.1 1.4 place_blocks.4.refs_2_
  138.5 2.4 %collective-permute-done.3.refs_1_ = bf16[32,8,512]{2,1,0:T(8,128)(2,1)S(1)} collective-permute-done((bf16[32,8,512]{2,1,0:T(8,128)(2,1)S(1)}, bf16[32,8,512]{2,1,0:T(8,128)(2,1)S(1)}, u32[]{:S(2)}, u32[]{:S(2)}) %collective-permute-start.3) | collective-permute-done | bytes 262176 | tf_op jit(solution)/shard_map/ppermute | solution.py:252
  140.9 1.8 %collective-permute-done.1.refs_0_ = bf16[32,8,512]{2,1,0:T(8,128)(2,1)S(1)} collective-permute-done((bf16[32,8,512]{2,1,0:T(8,128)(2,1)S(1)}, bf16[32,8,512]{2,1,0:T(8,128)(2,1)S(1)}, u32[]{:S(2)}, u32[]{:S(2)}) %collective-permute-start.1) | collective-permute-done | bytes 262176 | tf_op jit(solution)/shard_map/ppermute | solution.py:252
  142.7 1.4 place_blocks.5
  (1 shorter events, 0.0 us)
Async XLA Ops:
  0.6 1.6 %copy-start = (bf16[1,256,8,512]{3,2,1,0:T(8,128)(2,1)S(1)}, bf16[1,256,8,512]{3,2,1,0:T(8,128)(2,1)}, u32[]{:S(2)}) copy-start(bf16[1,256,8,512]{3,2,1,0:T(8,128)(2,1)} %param.3) | copy-start | bytes 6291460
  4.3 69.2 %all-to-all-start = ((bf16[256,8,512]{2,1,0:T(8,128)(2,1)}), bf16[256,8,512]{2,1,0:T(8,128)(2,1)}, u32[]{:S(2)}, u32[]{:S(2)}) async-start(bf16[256,8,512]{2,1,0:T(8,128)(2,1)} %gather_fusion), calls=%async_computation | async-start | bytes 4194304 | tf_op jit(solution)/shard_map/all_to_all | solution.py:243
  21.0 1.6 %copy-start.2 = (f32[1,2,512,512]{3,2,1,0:T(8,128)S(1)}, f32[1,2,512,512]{3,2,1,0:T(8,128)}, u32[]{:S(2)}) copy-start(f32[1,2,512,512]{3,2,1,0:T(8,128)} %param.5) | copy-start | bytes 6291460
  26.0 1.3 copy-start.3
  27.3 1.3 copy-start.5
  73.5 1.6 %copy-start.4 = (bf16[2,2,512,512]{3,2,1,0:T(8,128)(2,1)S(1)}, bf16[2,2,512,512]{3,2,1,0:T(8,128)(2,1)}, u32[]{:S(2)}) copy-start(bf16[2,2,512,512]{3,2,1,0:T(8,128)(2,1)} %copy-done.3) | copy-start | bytes 6291460
  75.1 1.6 %copy-start.6 = (bf16[2,2,512,512]{3,2,1,0:T(8,128)(2,1)S(1)}, bf16[2,2,512,512]{3,2,1,0:T(8,128)(2,1)}, u32[]{:S(2)}) copy-start(bf16[2,2,512,512]{3,2,1,0:T(8,128)(2,1)} %copy-done.5) | copy-start | bytes 6291460
  98.8 33.0 %copy-start.1 = (s32[256]{0:T(256)S(1)}, s32[256]{0:T(256)}, u32[]{:S(2)}) copy-start(s32[256]{0:T(256)} %order.5) | copy-start | bytes 3076
  122.1 7.6 %collective-permute-start.2 = (bf16[32,8,512]{2,1,0:T(8,128)(2,1)S(1)}, bf16[32,8,512]{2,1,0:T(8,128)(2,1)S(1)}, u32[]{:S(2)}, u32[]{:S(2)}) collective-permute-start(bf16[32,8,512]{2,1,0:T(8,128)(2,1)S(1)} %get-tuple-element.10), channel_id=1, source_target_pairs={{0,192},{64,0},{128,64},{192,128},{1,193},{65,1},{129,65},{193,129... | collective-permute-start | bytes 786440 | tf_op jit(solution)/shard_map/ppermute | solution.py:252
  123.1 8.7 %collective-permute-start = (bf16[32,8,512]{2,1,0:T(8,128)(2,1)S(1)}, bf16[32,8,512]{2,1,0:T(8,128)(2,1)S(1)}, u32[]{:S(2)}, u32[]{:S(2)}) collective-permute-start(bf16[32,8,512]{2,1,0:T(8,128)(2,1)S(1)} %get-tuple-element.11), channel_id=1, source_target_pairs={{0,64},{64,128},{128,192},{192,0},{1,65},{65,129},{129,193},{193,1... | collective-permute-start | bytes 786440 | tf_op jit(solution)/shard_map/ppermute | solution.py:252
  123.7 13.4 %collective-permute-start.4 = (bf16[32,8,512]{2,1,0:T(8,128)(2,1)S(1)}, bf16[32,8,512]{2,1,0:T(8,128)(2,1)S(1)}, u32[]{:S(2)}, u32[]{:S(2)}) collective-permute-start(bf16[32,8,512]{2,1,0:T(8,128)(2,1)S(1)} %get-tuple-element.10), channel_id=1, source_target_pairs={{0,64},{64,128},{128,192},{192,0},{1,65},{65,129},{129,193},{193,1... | collective-permute-start | bytes 786440 | tf_op jit(solution)/shard_map/ppermute | solution.py:252
  124.0 13.1 %collective-permute-start.5 = (bf16[32,8,512]{2,1,0:T(8,128)(2,1)S(1)}, bf16[32,8,512]{2,1,0:T(8,128)(2,1)S(1)}, u32[]{:S(2)}, u32[]{:S(2)}) collective-permute-start(bf16[32,8,512]{2,1,0:T(8,128)(2,1)S(1)} %get-tuple-element.11), channel_id=1, source_target_pairs={{0,192},{64,0},{128,64},{192,128},{1,193},{65,1},{129,65},{193,129... | collective-permute-start | bytes 786440 | tf_op jit(solution)/shard_map/ppermute | solution.py:252
  129.7 11.2 %collective-permute-start.3 = (bf16[32,8,512]{2,1,0:T(8,128)(2,1)S(1)}, bf16[32,8,512]{2,1,0:T(8,128)(2,1)S(1)}, u32[]{:S(2)}, u32[]{:S(2)}) collective-permute-start(bf16[32,8,512]{2,1,0:T(8,128)(2,1)S(1)} %collective-permute-done.2.refs_2_), channel_id=1, source_target_pairs={{0,192},{64,0},{128,64},{192,128},{1,193},{65,1},{129,65},{193,129... | collective-permute-start | bytes 786440 | tf_op jit(solution)/shard_map/ppermute | solution.py:252
  131.8 10.9 %collective-permute-start.1 = (bf16[32,8,512]{2,1,0:T(8,128)(2,1)S(1)}, bf16[32,8,512]{2,1,0:T(8,128)(2,1)S(1)}, u32[]{:S(2)}, u32[]{:S(2)}) collective-permute-start(bf16[32,8,512]{2,1,0:T(8,128)(2,1)S(1)} %collective-permute-done.refs_1_), channel_id=1, source_target_pairs={{0,64},{64,128},{128,192},{192,0},{1,65},{65,129},{129,193},{193,1... | collective-permute-start | bytes 786440 | tf_op jit(solution)/shard_map/ppermute | solution.py:252

commit v4 on v3

v4 whole, which is shorter than its diff:
```python
import functools

import jax
import jax.numpy as jnp
from jax import lax
from jax.experimental import pallas as pl
from jax.experimental.pallas import tpu as pltpu
from jax.sharding import PartitionSpec as P

MB = 1 << 20
PARTS = 2
BF16 = jnp.bfloat16
F32 = jnp.float32
ANY = pl.BlockSpec(memory_space=pl.ANY)
VMEM = pl.BlockSpec(memory_space=pltpu.VMEM)
SMEM = pl.BlockSpec(memory_space=pltpu.SMEM)


def split(value):
    high = value.astype(BF16)
    return high, (value - high.astype(F32)).astype(BF16)


def product3(lhs, rhs, rows):
    high = lhs[0, rows, :]
    left = jnp.concatenate([high, lhs[1, rows, :], high], axis=1)
    over = rhs[0]
    right = jnp.concatenate([over, over, rhs[1]], axis=0)
    return jnp.dot(left, right, preferred_element_type=F32)


def keep(target, rows, value):
    high, low = split(value)
    target[0, rows, :] = high
    target[1, rows, :] = low


def cut(width, count):
    size = width // count
    return [pl.ds(index * size, size) for index in range(count)]


def fourth_kernel(prev, out, square):
    x_out, q_out = out.at[0], out.at[1]
    width = prev.shape[-1]
    for side in range(2):
        keep(x_out.at[side], slice(None), prev[side])
    for source, target in ((x_out, square), (square, q_out)):
        for side in range(2):
            for rows in cut(width, PARTS):
                keep(target.at[side], rows, product3(source.at[side], source.at[side], rows))


def fourth_powers(prev):
    width = prev.shape[-1]
    return pl.pallas_call(
        fourth_kernel,
        out_shape=jax.ShapeDtypeStruct((2, 2, 2, width, width), BF16),
        in_specs=[VMEM],
        out_specs=VMEM,
        scratch_shapes=[pltpu.VMEM((2, 2, width, width), BF16)],
        compiler_params=pltpu.CompilerParams(vmem_limit_bytes=20 * MB),
        cost_estimate=pl.CostEstimate(
            flops=2 * 2 * 3 * 2 * width**3, bytes_accessed=6 * MB, transcendentals=0
        ),
        name="fourth_powers",
    )(prev)


def refresh_kernel(
    arrived, powers, roots, out,
    grads, x, q, stat, moment, factor, power, root, final, mean, mixed, sems,
):
    n_micro, width = grads.shape[0], grads.shape[-1]
    parts = cut(width, PARTS)
    size = width // PARTS
    batches = [pl.ds(0, n_micro // 2), pl.ds(n_micro // 2, n_micro // 2)]
    copies = [
        pltpu.make_async_copy(arrived.at[batch], grads.at[batch], sems.at[number])
        for number, batch in enumerate(batches)
    ]
    loads = [
        pltpu.make_async_copy(powers.at[1], q, sems.at[2]),
        pltpu.make_async_copy(powers.at[0], x, sems.at[3]),
    ]
    for copy in copies + loads:
        copy.start()
    for copy in copies:
        copy.wait()
    contracts = ((((1,), (1,)), ((), ())), (((0,), (0,)), ((), ())))
    scales = []
    whole = [grads[d] for d in range(n_micro)]
    for side in range(2):
        total = jnp.zeros((1, 1), F32)
        rhs = jnp.concatenate(whole, axis=1 - side)
        for index, rows in enumerate(parts):
            lo, hi = index * size, (index + 1) * size
            lhs = rhs[lo:hi, :] if side == 0 else rhs[:, lo:hi]
            value = lax.dot_general(lhs, rhs, contracts[side], preferred_element_type=F32)
            total = total + jnp.sum(value * value, axis=(0, 1), keepdims=True)
            keep(stat.at[side], rows, value)
        scales.append(1.0 / (jnp.sqrt(total / (width * width) + 1e-06) * width))

    row_ids = lax.broadcasted_iota(jnp.int32, (size, width), 0)
    col_ids = lax.broadcasted_iota(jnp.int32, (size, width), 1)

    def keep_factor(side, index, rows, value):
        diagonal = jnp.where(row_ids + index * size == col_ids, 1.25, 0.0)
        keep(factor.at[side], rows, diagonal - 0.25 * value)

    def five_quarters(side, rows):
        return 1.25 * (factor[side, 0, rows, :].astype(F32) + factor[side, 1, rows, :].astype(F32))

    for index, rows in enumerate(parts):
        value = grads[0, rows, :].astype(F32)
        for d in range(1, n_micro):
            value = value + grads[d, rows, :].astype(F32)
        keep(mean, rows, value / n_micro)
    for copy in loads:
        copy.wait()
    for index, rows in enumerate(parts):
        for side in range(2):
            value = product3(q.at[side], stat.at[side], rows) * scales[side]
            keep(moment.at[side], rows, value)
            keep_factor(side, index, rows, value)
    for rows in parts:
        for side in range(2):
            keep(power.at[0, side], rows, product3(factor.at[side], factor.at[side], rows))
    for rows in parts:
        for side in range(2):
            keep(root.at[side], rows, product3(x.at[side], factor.at[side], rows))
    for rows in parts:
        for side in range(2):
            keep(power.at[1, side], rows, product3(power.at[0, side], power.at[0, side], rows))
    for index, rows in enumerate(parts):
        for side in range(2):
            keep_factor(side, index, rows, product3(power.at[1, side], moment.at[side], rows))
    for rows in parts:
        for side in range(2):
            value = product3(factor.at[side], factor.at[side], rows)
            keep(power.at[0, side], rows, value)
            keep(power.at[1, side], rows, value - five_quarters(side, rows))
    for rows in parts:
        for side in range(2):
            keep(moment.at[side], rows, product3(power.at[0, side], power.at[1, side], rows))
    for rows in parts:
        for side in range(2):
            value = product3(power.at[0, side], moment.at[side], rows)
            keep(stat.at[side], rows, value + five_quarters(side, rows))
    last = power.at[1]
    writes = []
    for side in range(2):
        for rows in parts:
            value = product3(root.at[side], stat.at[side], rows)
            final[side, rows, :] = value
            keep(last.at[side], rows, value)
        write = pltpu.make_async_copy(final.at[side], roots.at[side], sems.at[side])
        write.start()
        writes.append(write)
    for rows in cut(width, 2):
        keep(mixed, rows, product3(last.at[0], mean, rows))
    for rows in cut(width, 2):
        out[rows, :] = product3(mixed, last.at[1], rows).astype(BF16)
    for write in writes:
        write.wait()


def refresh(arrived, powers):
    n_micro, width = arrived.shape[0], arrived.shape[-1]
    matrix = (2, 2, width, width)
    return pl.pallas_call(
        refresh_kernel,
        out_shape=(
            jax.ShapeDtypeStruct((2, width, width), F32),
            jax.ShapeDtypeStruct((width, width), BF16),
        ),
        in_specs=[ANY, ANY],
        out_specs=(ANY, VMEM),
        scratch_shapes=[
            pltpu.VMEM((n_micro, width, width), BF16),
            pltpu.VMEM(matrix, BF16),
            pltpu.VMEM(matrix, BF16),
            pltpu.VMEM(matrix, BF16),
            pltpu.VMEM(matrix, BF16),
            pltpu.VMEM(matrix, BF16),
            pltpu.VMEM((2,) + matrix, BF16),
            pltpu.VMEM(matrix, BF16),
            pltpu.VMEM((2, width, width), F32),
            pltpu.VMEM((2, width, width), BF16),
            pltpu.VMEM((2, width, width), BF16),
            pltpu.SemaphoreType.DMA((4,)),
        ],
        compiler_params=pltpu.CompilerParams(vmem_limit_bytes=59 * MB),
        cost_estimate=pl.CostEstimate(
            flops=(20 * 3 + 8) * 2 * width**3, bytes_accessed=9 * MB, transcendentals=0
        ),
        name="refresh_roots",
    )(arrived, powers)


def place_kernel(owners, offsets, order, *refs):
    pieces, (out, sems) = refs[: len(offsets)], refs[-2:]
    n_data, mine = lax.axis_size("dp"), lax.axis_index("dp")
    for number, (piece, (by, skip)) in enumerate(zip(pieces, offsets)):
        base = lax.rem(mine + by, n_data) * owners + skip
        for i in range(piece.shape[0]):
            pltpu.make_async_copy(
                piece.at[i], out.at[order[base + i]], sems.at[number]
            ).start()
    for number, piece in enumerate(pieces):
        pltpu.make_async_copy(piece, out.at[pl.ds(0, piece.shape[0])], sems.at[number]).wait()


def place(owners, order, batch, base):
    offsets, pieces = zip(*batch)
    rows, width = pieces[0].shape[1:]
    count = len(pieces)
    args, specs, aliases = [order, *pieces], [SMEM] + [VMEM] * count, {}
    if base is not None:
        args.append(base)
        specs.append(ANY)
        aliases = {count + 1: 0}
    return pl.pallas_call(
        functools.partial(place_kernel, owners, offsets),
        out_shape=jax.ShapeDtypeStruct((order.shape[0], rows, width), BF16),
        in_specs=specs,
        out_specs=ANY,
        scratch_shapes=[pltpu.SemaphoreType.DMA((count,))],
        input_output_aliases=aliases,
        compiler_params=pltpu.CompilerParams(vmem_limit_bytes=8 * MB),
        cost_estimate=pl.CostEstimate(
            flops=0, bytes_accessed=4 * sum(p.size for p in pieces), transcendentals=0
        ),
        name="place_blocks",
    )(*args)


def body(grads, order, prev_roots):
    n_data = lax.axis_size("dp")
    local = grads[0]
    rows, width = local.shape[1:]
    outgoing = local.at[order].get(
        mode="promise_in_bounds", unique_indices=True, wrap_negative_indices=False
    )
    arrived = lax.all_to_all(outgoing, ("dp", "fsdp"), split_axis=0, concat_axis=0, tiled=True)
    powers = fourth_powers(prev_roots[0])
    roots, refreshed = refresh(arrived.reshape(n_data, width, width), powers)
    pieces = refreshed.reshape(width // rows, rows, width)
    mine = lax.all_to_all(pieces, "fsdp", split_axis=0, concat_axis=0, tiled=True)
    owners = mine.shape[0]
    half = owners // 2

    def shift(value, by):
        return lax.ppermute(value, "dp", [(i, (i + by) % n_data) for i in range(n_data)])

    low, high = mine[:half], mine[half:]
    low_up, high_down = shift(low, 1), shift(high, -1)
    high_up, low_down = shift(high, 1), shift(low, -1)
    low_far, high_far = shift(low_up, 1), shift(high_down, -1)
    result = None
    for batch in (
        (((0, 0), mine), ((n_data - 1, 0), low_up), ((1, half), high_down)),
        (((n_data - 1, half), high_up), ((1, 0), low_down)),
        (((n_data - 2, 0), low_far), ((2, half), high_far)),
    ):
        result = place(owners, order, batch, result)
    return (result, roots[None])


def solution(mesh):
    return jax.shard_map(
        body,
        mesh=mesh,
        in_specs=(P("dp", None, "fsdp", None), P(), P(("dp", "fsdp"), None, None, None)),
        out_specs=(P(None, "fsdp", None), P(("dp", "fsdp"), None, None, None)),
        check_vma=False,
    )
```

time: 145 us -> 142 us (0.979)
  local copies, waits for them, and re-layouts: 10.3 us -> 6.41 us
    unnamed x14 -> x8, local copies, waits for them, and re-layouts: 8.18 us -> 4.3 us
where the time goes in v4:
time: 142 us; the launch traced here: 141 us
  waiting for transfers between devices  56.6 us (40%)
  Pallas kernels  30.3 us (21%)
  blocking collectives  23.5 us (17%)
  starting transfers between devices  23 us (16%)
  local copies, waits for them, and re-layouts  6.41 us (5%)
    all_to_all x1, waiting for transfers between devices, body(): lax.all_to_all(outgoing, ('dp', 'fsdp'), split_axis=0, concat_axis=0, til...  45.5 us
    all_to_all x1, blocking collectives, body(): lax.all_to_all(pieces, 'fsdp', split_axis=0, concat_axis=0, tiled=True)  23.5 us
    pallas_call x1, Pallas kernels, refresh(): pl.pallas_call(refresh_kernel, out_shape=(jax.ShapeDtypeStruct((2, width,...  22.3 us
    all_to_all x1, starting transfers between devices, body(): lax.all_to_all(outgoing, ('dp', 'fsdp'), split_axis=0, concat_axis=0, til...  16.7 us
    ppermute x6, waiting for transfers between devices, shift(): lax.ppermute(value, 'dp', [(i, (i + by) % n_data) for i in range(n_data)])  11.2 us
    ppermute x6, starting transfers between devices, shift(): lax.ppermute(value, 'dp', [(i, (i + by) % n_data) for i in range(n_data)])  6.32 us
    pallas_call x3, Pallas kernels, place(): pl.pallas_call(functools.partial(place_kernel, owners, offsets), out_shap...  4.48 us
    unnamed x8, local copies, waits for them, and re-layouts  4.3 us
  transfers between devices with their start and end apart: 7, of which 5 were waited for; matrix products, arithmetic and copies ran while one was open for 0% of the time, Pallas kernels for 5%

profile of v4, /device:TPU:1, one launch (start us, length us, event | category | flops | bytes accessed | tf_op | source)
XLA Modules:
  0.0 141.5 jit_solution(11642810456733398460)
XLA Ops:
  0.6 0.0 copy-start
  0.6 0.8 pad_clamp_fusion
  1.5 0.8 copy-done
  2.2 2.1 %gather_fusion = bf16[256,8,512]{2,1,0:T(8,128)(2,1)} fusion(bf16[256,8,512]{2,1,0:T(8,128)(2,1)S(1)} %bitcast.5, s32[1024]{0:T(1024)S(1)} %pad_clamp_fusion), kind=kCustom, calls=%fused_computation | custom fusion | bytes 4195328 | tf_op jit(solution)/shard_map/gather | solution.py:242
  4.3 16.7 %all-to-all-start = ((bf16[256,8,512]{2,1,0:T(8,128)(2,1)}), bf16[256,8,512]{2,1,0:T(8,128)(2,1)}, u32[]{:S(2)}, u32[]{:S(2)}) async-start(bf16[256,8,512]{2,1,0:T(8,128)(2,1)} %gather_fusion), calls=%async_computation | async-start | bytes 4194304 | tf_op jit(solution)/shard_map/all_to_all | solution.py:245
  21.0 0.0 copy-start.2
  21.0 1.6 %copy-done.2 = f32[1,2,512,512]{3,2,1,0:T(8,128)S(1)} copy-done((f32[1,2,512,512]{3,2,1,0:T(8,128)S(1)}, f32[1,2,512,512]{3,2,1,0:T(8,128)}, u32[]{:S(2)}) %copy-start.2) | copy-done | bytes 2097176
  22.6 3.5 %fourth_powers.1.powers = bf16[2,2,2,512,512]{4,3,2,1,0:T(8,128)(2,1)S(1)} custom-call(f32[2,512,512]{2,1,0:T(8,128)S(1)} %bitcast.6), custom_call_target="tpu_custom_call" | custom-call | flops 3221225472 | bytes 6291456 | tf_op jit(solution)/shard_map/fourth_powers/pallas_call | solution.py:56
  26.1 0.0 copy-start.3
  26.1 1.9 %copy-done.3 = bf16[2,2,2,512,512]{4,3,2,1,0:T(8,128)(2,1)} copy-done((bf16[2,2,2,512,512]{4,3,2,1,0:T(8,128)(2,1)}, bf16[2,2,2,512,512]{4,3,2,1,0:T(8,128)(2,1)S(1)}, u32[]{:S(2)}) %copy-start.3) | copy-done | bytes 4194328
  28.0 45.5 %all-to-all-done = bf16[256,8,512]{2,1,0:T(8,128)(2,1)} async-done(((bf16[256,8,512]{2,1,0:T(8,128)(2,1)}), bf16[256,8,512]{2,1,0:T(8,128)(2,1)}, u32[]{:S(2)}, u32[]{:S(2)}) %all-to-all-start) | async-done | bytes 2097184 | tf_op jit(solution)/shard_map/all_to_all | solution.py:245
  73.5 22.3 %refresh_roots.1 = (f32[2,512,512]{2,1,0:T(8,128)}, bf16[512,512]{1,0:T(8,128)(2,1)}) custom-call(bf16[4,512,512]{2,1,0:T(8,128)(2,1)} %bitcast.1.arrived, bf16[2,2,2,512,512]{4,3,2,1,0:T(8,128)(2,1)} %copy-done.3), custom_call_target="tpu_custom_call" | custom-call | flops 18253611008 | bytes 9437184 | tf_op jit(solution)/shard_map/refresh_roots/pallas_call | solution.py:171
  95.8 0.0 copy-start.1
  95.8 23.5 %all_to_all.10.refs_0_ = bf16[64,8,512]{2,1,0:T(8,128)(2,1)S(1)} all-to-all(bf16[64,8,512]{2,1,0:T(8,128)(2,1)} %bitcast.7), channel_id=1, replica_groups=mesh['dp'=4,'fsdp'=64] {'fsdp'}, dimensions={0} | all-to-all | bytes 1048576 | tf_op jit(solution)/shard_map/all_to_all | solution.py:249
  119.3 1.0 collective-permute-start.2
  120.3 0.6 collective-permute-start
  120.9 0.3 collective-permute-start.4
  121.2 2.4 %collective-permute-start.5 = (bf16[32,8,512]{2,1,0:T(8,128)(2,1)S(1)}, bf16[32,8,512]{2,1,0:T(8,128)(2,1)S(1)}, u32[]{:S(2)}, u32[]{:S(2)}) collective-permute-start(bf16[32,8,512]{2,1,0:T(8,128)(2,1)S(1)} %get-tuple-element.7), channel_id=1, source_target_pairs={{0,192},{64,0},{128,64},{192,128},{1,193},{65,1},{129,65},{193,129... | collective-permute-start | bytes 786440 | tf_op jit(solution)/shard_map/ppermute | solution.py:254
  123.6 3.3 %collective-permute-done.2.refs_2_ = bf16[32,8,512]{2,1,0:T(8,128)(2,1)S(1)} collective-permute-done((bf16[32,8,512]{2,1,0:T(8,128)(2,1)S(1)}, bf16[32,8,512]{2,1,0:T(8,128)(2,1)S(1)}, u32[]{:S(2)}, u32[]{:S(2)}) %collective-permute-start.2) | collective-permute-done | bytes 262176 | tf_op jit(solution)/shard_map/ppermute | solution.py:254
  126.9 2.1 %collective-permute-start.3 = (bf16[32,8,512]{2,1,0:T(8,128)(2,1)S(1)}, bf16[32,8,512]{2,1,0:T(8,128)(2,1)S(1)}, u32[]{:S(2)}, u32[]{:S(2)}) collective-permute-start(bf16[32,8,512]{2,1,0:T(8,128)(2,1)S(1)} %collective-permute-done.2.refs_2_), channel_id=1, source_target_pairs={{0,192},{64,0},{128,64},{192,128},{1,193},{65,1},{129,65},{193,129... | collective-permute-start | bytes 786440 | tf_op jit(solution)/shard_map/ppermute | solution.py:254
  129.0 0.0 collective-permute-done.refs_1_
  129.0 0.0 collective-permute-start.1
  129.0 0.0 copy-done.1
  129.0 1.7 %place_blocks.3.refs_2_ = bf16[256,8,512]{2,1,0:T(8,128)(2,1)} custom-call(s32[256]{0:T(256)S(1)} %copy-done.1, bf16[64,8,512]{2,1,0:T(8,128)(2,1)S(1)} %all_to_all.10.refs_0_, bf16[32,8,512]{2,1,0:T(8,128)(2,1)S(1)} %collective-permute-done.refs_1_, bf16[32,8,512]{2,1,0:T(8,128)(2,1)S(1)} %collective-permute-done.2.refs_2_), custom_call_target="tpu_custom_call" | custom-call | bytes 2097152 | tf_op jit(solution)/shard_map/place_blocks/pallas_call | solution.py:223
  130.7 3.6 %collective-permute-done.4.refs_0_ = bf16[32,8,512]{2,1,0:T(8,128)(2,1)S(1)} collective-permute-done((bf16[32,8,512]{2,1,0:T(8,128)(2,1)S(1)}, bf16[32,8,512]{2,1,0:T(8,128)(2,1)S(1)}, u32[]{:S(2)}, u32[]{:S(2)}) %collective-permute-start.4) | collective-permute-done | bytes 262176 | tf_op jit(solution)/shard_map/ppermute | solution.py:254
  134.3 0.0 collective-permute-done.5.refs_1_
  134.3 1.4 place_blocks.4.refs_2_
  135.7 2.4 %collective-permute-done.3.refs_1_ = bf16[32,8,512]{2,1,0:T(8,128)(2,1)S(1)} collective-permute-done((bf16[32,8,512]{2,1,0:T(8,128)(2,1)S(1)}, bf16[32,8,512]{2,1,0:T(8,128)(2,1)S(1)}, u32[]{:S(2)}, u32[]{:S(2)}) %collective-permute-start.3) | collective-permute-done | bytes 262176 | tf_op jit(solution)/shard_map/ppermute | solution.py:254
  138.1 1.8 %collective-permute-done.1.refs_0_ = bf16[32,8,512]{2,1,0:T(8,128)(2,1)S(1)} collective-permute-done((bf16[32,8,512]{2,1,0:T(8,128)(2,1)S(1)}, bf16[32,8,512]{2,1,0:T(8,128)(2,1)S(1)}, u32[]{:S(2)}, u32[]{:S(2)}) %collective-permute-start.1) | collective-permute-done | bytes 262176 | tf_op jit(solution)/shard_map/ppermute | solution.py:254
  139.9 1.4 place_blocks.5
  (1 shorter events, 0.0 us)
Async XLA Ops:
  0.6 1.6 %copy-start = (bf16[1,256,8,512]{3,2,1,0:T(8,128)(2,1)S(1)}, bf16[1,256,8,512]{3,2,1,0:T(8,128)(2,1)}, u32[]{:S(2)}) copy-start(bf16[1,256,8,512]{3,2,1,0:T(8,128)(2,1)} %param.3) | copy-start | bytes 6291460
  4.3 69.2 %all-to-all-start = ((bf16[256,8,512]{2,1,0:T(8,128)(2,1)}), bf16[256,8,512]{2,1,0:T(8,128)(2,1)}, u32[]{:S(2)}, u32[]{:S(2)}) async-start(bf16[256,8,512]{2,1,0:T(8,128)(2,1)} %gather_fusion), calls=%async_computation | async-start | bytes 4194304 | tf_op jit(solution)/shard_map/all_to_all | solution.py:245
  21.0 1.6 %copy-start.2 = (f32[1,2,512,512]{3,2,1,0:T(8,128)S(1)}, f32[1,2,512,512]{3,2,1,0:T(8,128)}, u32[]{:S(2)}) copy-start(f32[1,2,512,512]{3,2,1,0:T(8,128)} %param.5) | copy-start | bytes 6291460
  26.1 1.9 %copy-start.3 = (bf16[2,2,2,512,512]{4,3,2,1,0:T(8,128)(2,1)}, bf16[2,2,2,512,512]{4,3,2,1,0:T(8,128)(2,1)S(1)}, u32[]{:S(2)}) copy-start(bf16[2,2,2,512,512]{4,3,2,1,0:T(8,128)(2,1)S(1)} %fourth_powers.1.powers) | copy-start | bytes 12582916
  95.8 33.2 %copy-start.1 = (s32[256]{0:T(256)S(1)}, s32[256]{0:T(256)}, u32[]{:S(2)}) copy-start(s32[256]{0:T(256)} %order.5) | copy-start | bytes 3076
  119.3 7.6 %collective-permute-start.2 = (bf16[32,8,512]{2,1,0:T(8,128)(2,1)S(1)}, bf16[32,8,512]{2,1,0:T(8,128)(2,1)S(1)}, u32[]{:S(2)}, u32[]{:S(2)}) collective-permute-start(bf16[32,8,512]{2,1,0:T(8,128)(2,1)S(1)} %get-tuple-element.6), channel_id=1, source_target_pairs={{0,192},{64,0},{128,64},{192,128},{1,193},{65,1},{129,65},{193,129... | collective-permute-start | bytes 786440 | tf_op jit(solution)/shard_map/ppermute | solution.py:254
  120.3 8.7 %collective-permute-start = (bf16[32,8,512]{2,1,0:T(8,128)(2,1)S(1)}, bf16[32,8,512]{2,1,0:T(8,128)(2,1)S(1)}, u32[]{:S(2)}, u32[]{:S(2)}) collective-permute-start(bf16[32,8,512]{2,1,0:T(8,128)(2,1)S(1)} %get-tuple-element.7), channel_id=1, source_target_pairs={{0,64},{64,128},{128,192},{192,0},{1,65},{65,129},{129,193},{193,1... | collective-permute-start | bytes 786440 | tf_op jit(solution)/shard_map/ppermute | solution.py:254
  120.9 13.4 %collective-permute-start.4 = (bf16[32,8,512]{2,1,0:T(8,128)(2,1)S(1)}, bf16[32,8,512]{2,1,0:T(8,128)(2,1)S(1)}, u32[]{:S(2)}, u32[]{:S(2)}) collective-permute-start(bf16[32,8,512]{2,1,0:T(8,128)(2,1)S(1)} %get-tuple-element.6), channel_id=1, source_target_pairs={{0,64},{64,128},{128,192},{192,0},{1,65},{65,129},{129,193},{193,1... | collective-permute-start | bytes 786440 | tf_op jit(solution)/shard_map/ppermute | solution.py:254
  121.2 13.1 %collective-permute-start.5 = (bf16[32,8,512]{2,1,0:T(8,128)(2,1)S(1)}, bf16[32,8,512]{2,1,0:T(8,128)(2,1)S(1)}, u32[]{:S(2)}, u32[]{:S(2)}) collective-permute-start(bf16[32,8,512]{2,1,0:T(8,128)(2,1)S(1)} %get-tuple-element.7), channel_id=1, source_target_pairs={{0,192},{64,0},{128,64},{192,128},{1,193},{65,1},{129,65},{193,129... | collective-permute-start | bytes 786440 | tf_op jit(solution)/shard_map/ppermute | solution.py:254
  126.9 11.2 %collective-permute-start.3 = (bf16[32,8,512]{2,1,0:T(8,128)(2,1)S(1)}, bf16[32,8,512]{2,1,0:T(8,128)(2,1)S(1)}, u32[]{:S(2)}, u32[]{:S(2)}) collective-permute-start(bf16[32,8,512]{2,1,0:T(8,128)(2,1)S(1)} %collective-permute-done.2.refs_2_), channel_id=1, source_target_pairs={{0,192},{64,0},{128,64},{192,128},{1,193},{65,1},{129,65},{193,129... | collective-permute-start | bytes 786440 | tf_op jit(solution)/shard_map/ppermute | solution.py:254
  129.0 10.9 %collective-permute-start.1 = (bf16[32,8,512]{2,1,0:T(8,128)(2,1)S(1)}, bf16[32,8,512]{2,1,0:T(8,128)(2,1)S(1)}, u32[]{:S(2)}, u32[]{:S(2)}) collective-permute-start(bf16[32,8,512]{2,1,0:T(8,128)(2,1)S(1)} %collective-permute-done.refs_1_), channel_id=1, source_target_pairs={{0,64},{64,128},{128,192},{192,0},{1,65},{65,129},{129,193},{193,1... | collective-permute-start | bytes 786440 | tf_op jit(solution)/shard_map/ppermute | solution.py:254

commit v5 on v4

--- a/solution.py
+++ b/solution.py
@@ -74,19 +74,19 @@
     n_micro, width = grads.shape[0], grads.shape[-1]
     parts = cut(width, PARTS)
     size = width // PARTS
-    batches = [pl.ds(0, n_micro // 2), pl.ds(n_micro // 2, n_micro // 2)]
     copies = [
-        pltpu.make_async_copy(arrived.at[batch], grads.at[batch], sems.at[number])
-        for number, batch in enumerate(batches)
+        pltpu.make_async_copy(arrived.at[d], grads.at[d], sems.at[d]) for d in range(n_micro)
     ]
     loads = [
-        pltpu.make_async_copy(powers.at[1], q, sems.at[2]),
-        pltpu.make_async_copy(powers.at[0], x, sems.at[3]),
+        pltpu.make_async_copy(powers.at[1], q, sems.at[n_micro]),
+        pltpu.make_async_copy(powers.at[0], x, sems.at[n_micro + 1]),
     ]
-    for copy in copies + loads:
+    for copy in copies:
         copy.start()
     for copy in copies:
         copy.wait()
+    for copy in loads:
+        copy.start()
     contracts = ((((1,), (1,)), ((), ())), (((0,), (0,)), ((), ())))
     scales = []
     whole = [grads[d] for d in range(n_micro)]
@@ -116,8 +116,7 @@
         for d in range(1, n_micro):
             value = value + grads[d, rows, :].astype(F32)
         keep(mean, rows, value / n_micro)
-    for copy in loads:
-        copy.wait()
+    loads[0].wait()
     for index, rows in enumerate(parts):
         for side in range(2):
             value = product3(q.at[side], stat.at[side], rows) * scales[side]
@@ -126,6 +125,7 @@
     for rows in parts:
         for side in range(2):
             keep(power.at[0, side], rows, product3(factor.at[side], factor.at[side], rows))
+    loads[1].wait()
     for rows in parts:
         for side in range(2):
             keep(root.at[side], rows, product3(x.at[side], factor.at[side], rows))
@@ -188,9 +188,9 @@
             pltpu.VMEM((2, width, width), F32),
             pltpu.VMEM((2, width, width), BF16),
             pltpu.VMEM((2, width, width), BF16),
-            pltpu.SemaphoreType.DMA((4,)),
+            pltpu.SemaphoreType.DMA((n_micro + 2,)),
         ],
-        compiler_params=pltpu.CompilerParams(vmem_limit_bytes=59 * MB),
+        compiler_params=pltpu.CompilerParams(vmem_limit_bytes=53 * MB),
         cost_estimate=pl.CostEstimate(
             flops=(20 * 3 + 8) * 2 * width**3, bytes_accessed=9 * MB, transcendentals=0
         ),

time: 142 us -> 141 us (level)
  no operation moved by 1% of the time
where the time goes in v5:
time: 141 us
  waiting for transfers between devices  56.6 us (40%)
  Pallas kernels  29.6 us (21%)
  blocking collectives  23.2 us (16%)
  starting transfers between devices  23 us (16%)
  local copies, waits for them, and re-layouts  6.41 us (5%)
    all_to_all x1, waiting for transfers between devices, body(): lax.all_to_all(outgoing, ('dp', 'fsdp'), split_axis=0, concat_axis=0, til...  45.5 us
    all_to_all x1, blocking collectives, body(): lax.all_to_all(pieces, 'fsdp', split_axis=0, concat_axis=0, tiled=True)  23.2 us
    pallas_call x1, Pallas kernels, refresh(): pl.pallas_call(refresh_kernel, out_shape=(jax.ShapeDtypeStruct((2, width,...  21.7 us
    all_to_all x1, starting transfers between devices, body(): lax.all_to_all(outgoing, ('dp', 'fsdp'), split_axis=0, concat_axis=0, til...  16.7 us
    ppermute x6, waiting for transfers between devices, shift(): lax.ppermute(value, 'dp', [(i, (i + by) % n_data) for i in range(n_data)])  11.2 us
    ppermute x6, starting transfers between devices, shift(): lax.ppermute(value, 'dp', [(i, (i + by) % n_data) for i in range(n_data)])  6.32 us
    pallas_call x3, Pallas kernels, place(): pl.pallas_call(functools.partial(place_kernel, owners, offsets), out_shap...  4.48 us
    unnamed x8, local copies, waits for them, and re-layouts  4.3 us
  transfers between devices with their start and end apart: 7, of which 5 were waited for; matrix products, arithmetic and copies ran while one was open for 0% of the time, Pallas kernels for 5%

profile of v5, /device:TPU:1, one launch (start us, length us, event | category | flops | bytes accessed | tf_op | source)
XLA Modules:
  0.0 140.6 jit_solution(6711994323732048894)
XLA Ops:
  0.6 0.0 copy-start
  0.6 0.8 pad_clamp_fusion
  1.5 0.8 copy-done
  2.2 2.1 %gather_fusion = bf16[256,8,512]{2,1,0:T(8,128)(2,1)} fusion(bf16[256,8,512]{2,1,0:T(8,128)(2,1)S(1)} %bitcast.5, s32[1024]{0:T(1024)S(1)} %pad_clamp_fusion), kind=kCustom, calls=%fused_computation | custom fusion | bytes 4195328 | tf_op jit(solution)/shard_map/gather | solution.py:242
  4.3 16.7 %all-to-all-start = ((bf16[256,8,512]{2,1,0:T(8,128)(2,1)}), bf16[256,8,512]{2,1,0:T(8,128)(2,1)}, u32[]{:S(2)}, u32[]{:S(2)}) async-start(bf16[256,8,512]{2,1,0:T(8,128)(2,1)} %gather_fusion), calls=%async_computation | async-start | bytes 4194304 | tf_op jit(solution)/shard_map/all_to_all | solution.py:245
  21.0 0.0 copy-start.2
  21.0 1.6 %copy-done.2 = f32[1,2,512,512]{3,2,1,0:T(8,128)S(1)} copy-done((f32[1,2,512,512]{3,2,1,0:T(8,128)S(1)}, f32[1,2,512,512]{3,2,1,0:T(8,128)}, u32[]{:S(2)}) %copy-start.2) | copy-done | bytes 2097176
  22.6 3.5 %fourth_powers.1.powers = bf16[2,2,2,512,512]{4,3,2,1,0:T(8,128)(2,1)S(1)} custom-call(f32[2,512,512]{2,1,0:T(8,128)S(1)} %bitcast.7), custom_call_target="tpu_custom_call" | custom-call | flops 3221225472 | bytes 6291456 | tf_op jit(solution)/shard_map/fourth_powers/pallas_call | solution.py:56
  26.1 0.0 copy-start.3
  26.1 1.9 %copy-done.3 = bf16[2,2,2,512,512]{4,3,2,1,0:T(8,128)(2,1)} copy-done((bf16[2,2,2,512,512]{4,3,2,1,0:T(8,128)(2,1)}, bf16[2,2,2,512,512]{4,3,2,1,0:T(8,128)(2,1)S(1)}, u32[]{:S(2)}) %copy-start.3) | copy-done | bytes 4194328
  28.0 45.5 %all-to-all-done = bf16[256,8,512]{2,1,0:T(8,128)(2,1)} async-done(((bf16[256,8,512]{2,1,0:T(8,128)(2,1)}), bf16[256,8,512]{2,1,0:T(8,128)(2,1)}, u32[]{:S(2)}, u32[]{:S(2)}) %all-to-all-start) | async-done | bytes 2097184 | tf_op jit(solution)/shard_map/all_to_all | solution.py:245
  73.5 21.7 %refresh_roots.1 = (f32[2,512,512]{2,1,0:T(8,128)}, bf16[512,512]{1,0:T(8,128)(2,1)S(1)}) custom-call(bf16[4,512,512]{2,1,0:T(8,128)(2,1)} %bitcast.1.arrived, bf16[2,2,2,512,512]{4,3,2,1,0:T(8,128)(2,1)} %copy-done.3), custom_call_target="tpu_custom_call" | custom-call | flops 18253611008 | bytes 9437184 | tf_op jit(solution)/shard_map/refresh_roots/pallas_call | solution.py:171
  95.1 0.0 copy-start.1
  95.2 23.2 %all_to_all.10.refs_0_ = bf16[64,8,512]{2,1,0:T(8,128)(2,1)S(1)} all-to-all(bf16[64,8,512]{2,1,0:T(8,128)(2,1)S(1)} %bitcast.6), channel_id=1, replica_groups=mesh['dp'=4,'fsdp'=64] {'fsdp'}, dimensions={0} | all-to-all | bytes 1048576 | tf_op jit(solution)/shard_map/all_to_all | solution.py:249
  118.4 1.0 collective-permute-start.2
  119.4 0.6 collective-permute-start
  120.0 0.3 collective-permute-start.4
  120.3 2.4 %collective-permute-start.5 = (bf16[32,8,512]{2,1,0:T(8,128)(2,1)S(1)}, bf16[32,8,512]{2,1,0:T(8,128)(2,1)S(1)}, u32[]{:S(2)}, u32[]{:S(2)}) collective-permute-start(bf16[32,8,512]{2,1,0:T(8,128)(2,1)S(1)} %get-tuple-element.7), channel_id=1, source_target_pairs={{0,192},{64,0},{128,64},{192,128},{1,193},{65,1},{129,65},{193,129... | collective-permute-start | bytes 786440 | tf_op jit(solution)/shard_map/ppermute | solution.py:254
  122.7 3.3 %collective-permute-done.2.refs_2_ = bf16[32,8,512]{2,1,0:T(8,128)(2,1)S(1)} collective-permute-done((bf16[32,8,512]{2,1,0:T(8,128)(2,1)S(1)}, bf16[32,8,512]{2,1,0:T(8,128)(2,1)S(1)}, u32[]{:S(2)}, u32[]{:S(2)}) %collective-permute-start.2) | collective-permute-done | bytes 262176 | tf_op jit(solution)/shard_map/ppermute | solution.py:254
  126.0 2.1 %collective-permute-start.3 = (bf16[32,8,512]{2,1,0:T(8,128)(2,1)S(1)}, bf16[32,8,512]{2,1,0:T(8,128)(2,1)S(1)}, u32[]{:S(2)}, u32[]{:S(2)}) collective-permute-start(bf16[32,8,512]{2,1,0:T(8,128)(2,1)S(1)} %collective-permute-done.2.refs_2_), channel_id=1, source_target_pairs={{0,192},{64,0},{128,64},{192,128},{1,193},{65,1},{129,65},{193,129... | collective-permute-start | bytes 786440 | tf_op jit(solution)/shard_map/ppermute | solution.py:254
  128.1 0.0 collective-permute-done.refs_1_
  128.1 0.0 collective-permute-start.1
  128.1 0.0 copy-done.1
  128.1 1.7 %place_blocks.3.refs_2_ = bf16[256,8,512]{2,1,0:T(8,128)(2,1)} custom-call(s32[256]{0:T(256)S(1)} %copy-done.1, bf16[64,8,512]{2,1,0:T(8,128)(2,1)S(1)} %all_to_all.10.refs_0_, bf16[32,8,512]{2,1,0:T(8,128)(2,1)S(1)} %collective-permute-done.refs_1_, bf16[32,8,512]{2,1,0:T(8,128)(2,1)S(1)} %collective-permute-done.2.refs_2_), custom_call_target="tpu_custom_call" | custom-call | bytes 2097152 | tf_op jit(solution)/shard_map/place_blocks/pallas_call | solution.py:223
  129.8 3.6 %collective-permute-done.4.refs_0_ = bf16[32,8,512]{2,1,0:T(8,128)(2,1)S(1)} collective-permute-done((bf16[32,8,512]{2,1,0:T(8,128)(2,1)S(1)}, bf16[32,8,512]{2,1,0:T(8,128)(2,1)S(1)}, u32[]{:S(2)}, u32[]{:S(2)}) %collective-permute-start.4) | collective-permute-done | bytes 262176 | tf_op jit(solution)/shard_map/ppermute | solution.py:254
  133.4 0.0 collective-permute-done.5.refs_1_
  133.4 1.4 %place_blocks.4.refs_2_ = bf16[256,8,512]{2,1,0:T(8,128)(2,1)} custom-call(s32[256]{0:T(256)S(1)} %copy-done.1, bf16[32,8,512]{2,1,0:T(8,128)(2,1)S(1)} %collective-permute-done.4.refs_0_, bf16[32,8,512]{2,1,0:T(8,128)(2,1)S(1)} %collective-permute-done.5.refs_1_, bf16[256,8,512]{2,1,0:T(8,128)(2,1)} %place_blocks.3.refs_2_), custom_call_target="tpu_custom_call", output_to_operand_aliasing={{}: (3, {})} | custom-call | bytes 1048576 | tf_op jit(solution)/shard_map/place_blocks/pallas_call | solution.py:223
  134.8 2.4 %collective-permute-done.3.refs_1_ = bf16[32,8,512]{2,1,0:T(8,128)(2,1)S(1)} collective-permute-done((bf16[32,8,512]{2,1,0:T(8,128)(2,1)S(1)}, bf16[32,8,512]{2,1,0:T(8,128)(2,1)S(1)}, u32[]{:S(2)}, u32[]{:S(2)}) %collective-permute-start.3) | collective-permute-done | bytes 262176 | tf_op jit(solution)/shard_map/ppermute | solution.py:254
  137.3 1.8 %collective-permute-done.1.refs_0_ = bf16[32,8,512]{2,1,0:T(8,128)(2,1)S(1)} collective-permute-done((bf16[32,8,512]{2,1,0:T(8,128)(2,1)S(1)}, bf16[32,8,512]{2,1,0:T(8,128)(2,1)S(1)}, u32[]{:S(2)}, u32[]{:S(2)}) %collective-permute-start.1) | collective-permute-done | bytes 262176 | tf_op jit(solution)/shard_map/ppermute | solution.py:254
  139.0 1.4 %place_blocks.5 = bf16[256,8,512]{2,1,0:T(8,128)(2,1)} custom-call(s32[256]{0:T(256)S(1)} %copy-done.1, bf16[32,8,512]{2,1,0:T(8,128)(2,1)S(1)} %collective-permute-done.1.refs_0_, bf16[32,8,512]{2,1,0:T(8,128)(2,1)S(1)} %collective-permute-done.3.refs_1_, bf16[256,8,512]{2,1,0:T(8,128)(2,1)} %place_blocks.4.refs_2_), custom_call_target="tpu_custom_call", output_to_operand_aliasing={{}: (3, {})} | custom-call | bytes 1048576 | tf_op jit(solution)/shard_map/place_blocks/pallas_call | solution.py:223
  (1 shorter events, 0.0 us)
Async XLA Ops:
  0.6 1.6 %copy-start = (bf16[1,256,8,512]{3,2,1,0:T(8,128)(2,1)S(1)}, bf16[1,256,8,512]{3,2,1,0:T(8,128)(2,1)}, u32[]{:S(2)}) copy-start(bf16[1,256,8,512]{3,2,1,0:T(8,128)(2,1)} %param.3) | copy-start | bytes 6291460
  4.3 69.2 %all-to-all-start = ((bf16[256,8,512]{2,1,0:T(8,128)(2,1)}), bf16[256,8,512]{2,1,0:T(8,128)(2,1)}, u32[]{:S(2)}, u32[]{:S(2)}) async-start(bf16[256,8,512]{2,1,0:T(8,128)(2,1)} %gather_fusion), calls=%async_computation | async-start | bytes 4194304 | tf_op jit(solution)/shard_map/all_to_all | solution.py:245
  21.0 1.6 %copy-start.2 = (f32[1,2,512,512]{3,2,1,0:T(8,128)S(1)}, f32[1,2,512,512]{3,2,1,0:T(8,128)}, u32[]{:S(2)}) copy-start(f32[1,2,512,512]{3,2,1,0:T(8,128)} %param.5) | copy-start | bytes 6291460
  26.1 1.9 %copy-start.3 = (bf16[2,2,2,512,512]{4,3,2,1,0:T(8,128)(2,1)}, bf16[2,2,2,512,512]{4,3,2,1,0:T(8,128)(2,1)S(1)}, u32[]{:S(2)}) copy-start(bf16[2,2,2,512,512]{4,3,2,1,0:T(8,128)(2,1)S(1)} %fourth_powers.1.powers) | copy-start | bytes 12582916
  95.1 33.0 %copy-start.1 = (s32[256]{0:T(256)S(1)}, s32[256]{0:T(256)}, u32[]{:S(2)}) copy-start(s32[256]{0:T(256)} %order.5) | copy-start | bytes 3076
  118.4 7.6 %collective-permute-start.2 = (bf16[32,8,512]{2,1,0:T(8,128)(2,1)S(1)}, bf16[32,8,512]{2,1,0:T(8,128)(2,1)S(1)}, u32[]{:S(2)}, u32[]{:S(2)}) collective-permute-start(bf16[32,8,512]{2,1,0:T(8,128)(2,1)S(1)} %get-tuple-element.6), channel_id=1, source_target_pairs={{0,192},{64,0},{128,64},{192,128},{1,193},{65,1},{129,65},{193,129... | collective-permute-start | bytes 786440 | tf_op jit(solution)/shard_map/ppermute | solution.py:254
  119.4 8.7 %collective-permute-start = (bf16[32,8,512]{2,1,0:T(8,128)(2,1)S(1)}, bf16[32,8,512]{2,1,0:T(8,128)(2,1)S(1)}, u32[]{:S(2)}, u32[]{:S(2)}) collective-permute-start(bf16[32,8,512]{2,1,0:T(8,128)(2,1)S(1)} %get-tuple-element.7), channel_id=1, source_target_pairs={{0,64},{64,128},{128,192},{192,0},{1,65},{65,129},{129,193},{193,1... | collective-permute-start | bytes 786440 | tf_op jit(solution)/shard_map/ppermute | solution.py:254
  120.0 13.4 %collective-permute-start.4 = (bf16[32,8,512]{2,1,0:T(8,128)(2,1)S(1)}, bf16[32,8,512]{2,1,0:T(8,128)(2,1)S(1)}, u32[]{:S(2)}, u32[]{:S(2)}) collective-permute-start(bf16[32,8,512]{2,1,0:T(8,128)(2,1)S(1)} %get-tuple-element.6), channel_id=1, source_target_pairs={{0,64},{64,128},{128,192},{192,0},{1,65},{65,129},{129,193},{193,1... | collective-permute-start | bytes 786440 | tf_op jit(solution)/shard_map/ppermute | solution.py:254
  120.3 13.1 %collective-permute-start.5 = (bf16[32,8,512]{2,1,0:T(8,128)(2,1)S(1)}, bf16[32,8,512]{2,1,0:T(8,128)(2,1)S(1)}, u32[]{:S(2)}, u32[]{:S(2)}) collective-permute-start(bf16[32,8,512]{2,1,0:T(8,128)(2,1)S(1)} %get-tuple-element.7), channel_id=1, source_target_pairs={{0,192},{64,0},{128,64},{192,128},{1,193},{65,1},{129,65},{193,129... | collective-permute-start | bytes 786440 | tf_op jit(solution)/shard_map/ppermute | solution.py:254
  126.0 11.2 %collective-permute-start.3 = (bf16[32,8,512]{2,1,0:T(8,128)(2,1)S(1)}, bf16[32,8,512]{2,1,0:T(8,128)(2,1)S(1)}, u32[]{:S(2)}, u32[]{:S(2)}) collective-permute-start(bf16[32,8,512]{2,1,0:T(8,128)(2,1)S(1)} %collective-permute-done.2.refs_2_), channel_id=1, source_target_pairs={{0,192},{64,0},{128,64},{192,128},{1,193},{65,1},{129,65},{193,129... | collective-permute-start | bytes 786440 | tf_op jit(solution)/shard_map/ppermute | solution.py:254
  128.1 10.9 %collective-permute-start.1 = (bf16[32,8,512]{2,1,0:T(8,128)(2,1)S(1)}, bf16[32,8,512]{2,1,0:T(8,128)(2,1)S(1)}, u32[]{:S(2)}, u32[]{:S(2)}) collective-permute-start(bf16[32,8,512]{2,1,0:T(8,128)(2,1)S(1)} %collective-permute-done.refs_1_), channel_id=1, source_target_pairs={{0,64},{64,128},{128,192},{192,0},{1,65},{65,129},{129,193},{193,1... | collective-permute-start | bytes 786440 | tf_op jit(solution)/shard_map/ppermute | solution.py:254

commit v6 on v5

--- a/solution.py
+++ b/solution.py
@@ -8,7 +8,7 @@
 from jax.sharding import PartitionSpec as P
 
 MB = 1 << 20
-PARTS = 2
+PARTS = 1
 BF16 = jnp.bfloat16
 F32 = jnp.float32
 ANY = pl.BlockSpec(memory_space=pl.ANY)
@@ -116,7 +116,8 @@
         for d in range(1, n_micro):
             value = value + grads[d, rows, :].astype(F32)
         keep(mean, rows, value / n_micro)
-    loads[0].wait()
+    for copy in loads:
+        copy.wait()
     for index, rows in enumerate(parts):
         for side in range(2):
             value = product3(q.at[side], stat.at[side], rows) * scales[side]
@@ -125,7 +126,6 @@
     for rows in parts:
         for side in range(2):
             keep(power.at[0, side], rows, product3(factor.at[side], factor.at[side], rows))
-    loads[1].wait()
     for rows in parts:
         for side in range(2):
             keep(root.at[side], rows, product3(x.at[side], factor.at[side], rows))

time: 141 us -> 141 us (level)
  no operation moved by 1% of the time
where the time goes in v6:
time: 141 us
  waiting for transfers between devices  56.6 us (40%)
  Pallas kernels  29.9 us (21%)
  blocking collectives  23.3 us (17%)
  starting transfers between devices  23 us (16%)
  local copies, waits for them, and re-layouts  6.41 us (5%)
    all_to_all x1, waiting for transfers between devices, body(): lax.all_to_all(outgoing, ('dp', 'fsdp'), split_axis=0, concat_axis=0, til...  45.5 us
    all_to_all x1, blocking collectives, body(): lax.all_to_all(pieces, 'fsdp', split_axis=0, concat_axis=0, tiled=True)  23.3 us
    pallas_call x1, Pallas kernels, refresh(): pl.pallas_call(refresh_kernel, out_shape=(jax.ShapeDtypeStruct((2, width,...  22 us
    all_to_all x1, starting transfers between devices, body(): lax.all_to_all(outgoing, ('dp', 'fsdp'), split_axis=0, concat_axis=0, til...  16.7 us
    ppermute x6, waiting for transfers between devices, shift(): lax.ppermute(value, 'dp', [(i, (i + by) % n_data) for i in range(n_data)])  11.2 us
    ppermute x6, starting transfers between devices, shift(): lax.ppermute(value, 'dp', [(i, (i + by) % n_data) for i in range(n_data)])  6.32 us
    pallas_call x3, Pallas kernels, place(): pl.pallas_call(functools.partial(place_kernel, owners, offsets), out_shap...  4.48 us
    unnamed x8, local copies, waits for them, and re-layouts  4.3 us
  transfers between devices with their start and end apart: 7, of which 5 were waited for; matrix products, arithmetic and copies ran while one was open for 0% of the time, Pallas kernels for 5%

profile of v6, /device:TPU:1, one launch (start us, length us, event | category | flops | bytes accessed | tf_op | source)
XLA Modules:
  0.0 140.9 jit_solution(18237610102850112078)
XLA Ops:
  0.6 0.0 copy-start
  0.6 0.8 pad_clamp_fusion
  1.5 0.8 copy-done
  2.2 2.1 %gather_fusion = bf16[256,8,512]{2,1,0:T(8,128)(2,1)} fusion(bf16[256,8,512]{2,1,0:T(8,128)(2,1)S(1)} %bitcast.5, s32[1024]{0:T(1024)S(1)} %pad_clamp_fusion), kind=kCustom, calls=%fused_computation | custom fusion | bytes 4195328 | tf_op jit(solution)/shard_map/gather | solution.py:242
  4.3 16.7 %all-to-all-start = ((bf16[256,8,512]{2,1,0:T(8,128)(2,1)}), bf16[256,8,512]{2,1,0:T(8,128)(2,1)}, u32[]{:S(2)}, u32[]{:S(2)}) async-start(bf16[256,8,512]{2,1,0:T(8,128)(2,1)} %gather_fusion), calls=%async_computation | async-start | bytes 4194304 | tf_op jit(solution)/shard_map/all_to_all | solution.py:245
  21.0 0.0 copy-start.2
  21.0 1.6 %copy-done.2 = f32[1,2,512,512]{3,2,1,0:T(8,128)S(1)} copy-done((f32[1,2,512,512]{3,2,1,0:T(8,128)S(1)}, f32[1,2,512,512]{3,2,1,0:T(8,128)}, u32[]{:S(2)}) %copy-start.2) | copy-done | bytes 2097176
  22.6 3.5 %fourth_powers.1.powers = bf16[2,2,2,512,512]{4,3,2,1,0:T(8,128)(2,1)S(1)} custom-call(f32[2,512,512]{2,1,0:T(8,128)S(1)} %bitcast.7), custom_call_target="tpu_custom_call" | custom-call | flops 3221225472 | bytes 6291456 | tf_op jit(solution)/shard_map/fourth_powers/pallas_call | solution.py:56
  26.1 0.0 copy-start.3
  26.1 1.9 %copy-done.3 = bf16[2,2,2,512,512]{4,3,2,1,0:T(8,128)(2,1)} copy-done((bf16[2,2,2,512,512]{4,3,2,1,0:T(8,128)(2,1)}, bf16[2,2,2,512,512]{4,3,2,1,0:T(8,128)(2,1)S(1)}, u32[]{:S(2)}) %copy-start.3) | copy-done | bytes 4194328
  28.0 45.5 %all-to-all-done = bf16[256,8,512]{2,1,0:T(8,128)(2,1)} async-done(((bf16[256,8,512]{2,1,0:T(8,128)(2,1)}), bf16[256,8,512]{2,1,0:T(8,128)(2,1)}, u32[]{:S(2)}, u32[]{:S(2)}) %all-to-all-start) | async-done | bytes 2097184 | tf_op jit(solution)/shard_map/all_to_all | solution.py:245
  73.5 22.0 %refresh_roots.1 = (f32[2,512,512]{2,1,0:T(8,128)}, bf16[512,512]{1,0:T(8,128)(2,1)S(1)}) custom-call(bf16[4,512,512]{2,1,0:T(8,128)(2,1)} %bitcast.1.arrived, bf16[2,2,2,512,512]{4,3,2,1,0:T(8,128)(2,1)} %copy-done.3), custom_call_target="tpu_custom_call" | custom-call | flops 18253611008 | bytes 9437184 | tf_op jit(solution)/shard_map/refresh_roots/pallas_call | solution.py:171
  95.5 0.0 copy-start.1
  95.5 23.3 %all_to_all.10.refs_0_ = bf16[64,8,512]{2,1,0:T(8,128)(2,1)S(1)} all-to-all(bf16[64,8,512]{2,1,0:T(8,128)(2,1)S(1)} %bitcast.6), channel_id=1, replica_groups=mesh['dp'=4,'fsdp'=64] {'fsdp'}, dimensions={0} | all-to-all | bytes 1048576 | tf_op jit(solution)/shard_map/all_to_all | solution.py:249
  118.8 0.9 collective-permute-start.2
  119.7 0.6 collective-permute-start
  120.3 0.3 collective-permute-start.4
  120.6 2.4 %collective-permute-start.5 = (bf16[32,8,512]{2,1,0:T(8,128)(2,1)S(1)}, bf16[32,8,512]{2,1,0:T(8,128)(2,1)S(1)}, u32[]{:S(2)}, u32[]{:S(2)}) collective-permute-start(bf16[32,8,512]{2,1,0:T(8,128)(2,1)S(1)} %get-tuple-element.7), channel_id=1, source_target_pairs={{0,192},{64,0},{128,64},{192,128},{1,193},{65,1},{129,65},{193,129... | collective-permute-start | bytes 786440 | tf_op jit(solution)/shard_map/ppermute | solution.py:254
  123.0 3.3 %collective-permute-done.2.refs_2_ = bf16[32,8,512]{2,1,0:T(8,128)(2,1)S(1)} collective-permute-done((bf16[32,8,512]{2,1,0:T(8,128)(2,1)S(1)}, bf16[32,8,512]{2,1,0:T(8,128)(2,1)S(1)}, u32[]{:S(2)}, u32[]{:S(2)}) %collective-permute-start.2) | collective-permute-done | bytes 262176 | tf_op jit(solution)/shard_map/ppermute | solution.py:254
  126.3 2.1 %collective-permute-start.3 = (bf16[32,8,512]{2,1,0:T(8,128)(2,1)S(1)}, bf16[32,8,512]{2,1,0:T(8,128)(2,1)S(1)}, u32[]{:S(2)}, u32[]{:S(2)}) collective-permute-start(bf16[32,8,512]{2,1,0:T(8,128)(2,1)S(1)} %collective-permute-done.2.refs_2_), channel_id=1, source_target_pairs={{0,192},{64,0},{128,64},{192,128},{1,193},{65,1},{129,65},{193,129... | collective-permute-start | bytes 786440 | tf_op jit(solution)/shard_map/ppermute | solution.py:254
  128.4 0.0 collective-permute-done.refs_1_
  128.4 0.0 collective-permute-start.1
  128.4 0.0 copy-done.1
  128.4 1.7 %place_blocks.3.refs_2_ = bf16[256,8,512]{2,1,0:T(8,128)(2,1)} custom-call(s32[256]{0:T(256)S(1)} %copy-done.1, bf16[64,8,512]{2,1,0:T(8,128)(2,1)S(1)} %all_to_all.10.refs_0_, bf16[32,8,512]{2,1,0:T(8,128)(2,1)S(1)} %collective-permute-done.refs_1_, bf16[32,8,512]{2,1,0:T(8,128)(2,1)S(1)} %collective-permute-done.2.refs_2_), custom_call_target="tpu_custom_call" | custom-call | bytes 2097152 | tf_op jit(solution)/shard_map/place_blocks/pallas_call | solution.py:223
  130.1 3.6 %collective-permute-done.4.refs_0_ = bf16[32,8,512]{2,1,0:T(8,128)(2,1)S(1)} collective-permute-done((bf16[32,8,512]{2,1,0:T(8,128)(2,1)S(1)}, bf16[32,8,512]{2,1,0:T(8,128)(2,1)S(1)}, u32[]{:S(2)}, u32[]{:S(2)}) %collective-permute-start.4) | collective-permute-done | bytes 262176 | tf_op jit(solution)/shard_map/ppermute | solution.py:254
  133.7 0.0 collective-permute-done.5.refs_1_
  133.7 1.4 %place_blocks.4.refs_2_ = bf16[256,8,512]{2,1,0:T(8,128)(2,1)} custom-call(s32[256]{0:T(256)S(1)} %copy-done.1, bf16[32,8,512]{2,1,0:T(8,128)(2,1)S(1)} %collective-permute-done.4.refs_0_, bf16[32,8,512]{2,1,0:T(8,128)(2,1)S(1)} %collective-permute-done.5.refs_1_, bf16[256,8,512]{2,1,0:T(8,128)(2,1)} %place_blocks.3.refs_2_), custom_call_target="tpu_custom_call", output_to_operand_aliasing={{}: (3, {})} | custom-call | bytes 1048576 | tf_op jit(solution)/shard_map/place_blocks/pallas_call | solution.py:223
  135.1 2.4 %collective-permute-done.3.refs_1_ = bf16[32,8,512]{2,1,0:T(8,128)(2,1)S(1)} collective-permute-done((bf16[32,8,512]{2,1,0:T(8,128)(2,1)S(1)}, bf16[32,8,512]{2,1,0:T(8,128)(2,1)S(1)}, u32[]{:S(2)}, u32[]{:S(2)}) %collective-permute-start.3) | collective-permute-done | bytes 262176 | tf_op jit(solution)/shard_map/ppermute | solution.py:254
  137.6 1.8 %collective-permute-done.1.refs_0_ = bf16[32,8,512]{2,1,0:T(8,128)(2,1)S(1)} collective-permute-done((bf16[32,8,512]{2,1,0:T(8,128)(2,1)S(1)}, bf16[32,8,512]{2,1,0:T(8,128)(2,1)S(1)}, u32[]{:S(2)}, u32[]{:S(2)}) %collective-permute-start.1) | collective-permute-done | bytes 262176 | tf_op jit(solution)/shard_map/ppermute | solution.py:254
  139.3 1.4 %place_blocks.5 = bf16[256,8,512]{2,1,0:T(8,128)(2,1)} custom-call(s32[256]{0:T(256)S(1)} %copy-done.1, bf16[32,8,512]{2,1,0:T(8,128)(2,1)S(1)} %collective-permute-done.1.refs_0_, bf16[32,8,512]{2,1,0:T(8,128)(2,1)S(1)} %collective-permute-done.3.refs_1_, bf16[256,8,512]{2,1,0:T(8,128)(2,1)} %place_blocks.4.refs_2_), custom_call_target="tpu_custom_call", output_to_operand_aliasing={{}: (3, {})} | custom-call | bytes 1048576 | tf_op jit(solution)/shard_map/place_blocks/pallas_call | solution.py:223
  (1 shorter events, 0.0 us)
Async XLA Ops:
  0.6 1.6 %copy-start = (bf16[1,256,8,512]{3,2,1,0:T(8,128)(2,1)S(1)}, bf16[1,256,8,512]{3,2,1,0:T(8,128)(2,1)}, u32[]{:S(2)}) copy-start(bf16[1,256,8,512]{3,2,1,0:T(8,128)(2,1)} %param.3) | copy-start | bytes 6291460
  4.3 69.2 %all-to-all-start = ((bf16[256,8,512]{2,1,0:T(8,128)(2,1)}), bf16[256,8,512]{2,1,0:T(8,128)(2,1)}, u32[]{:S(2)}, u32[]{:S(2)}) async-start(bf16[256,8,512]{2,1,0:T(8,128)(2,1)} %gather_fusion), calls=%async_computation | async-start | bytes 4194304 | tf_op jit(solution)/shard_map/all_to_all | solution.py:245
  21.0 1.6 %copy-start.2 = (f32[1,2,512,512]{3,2,1,0:T(8,128)S(1)}, f32[1,2,512,512]{3,2,1,0:T(8,128)}, u32[]{:S(2)}) copy-start(f32[1,2,512,512]{3,2,1,0:T(8,128)} %param.5) | copy-start | bytes 6291460
  26.1 1.9 %copy-start.3 = (bf16[2,2,2,512,512]{4,3,2,1,0:T(8,128)(2,1)}, bf16[2,2,2,512,512]{4,3,2,1,0:T(8,128)(2,1)S(1)}, u32[]{:S(2)}) copy-start(bf16[2,2,2,512,512]{4,3,2,1,0:T(8,128)(2,1)S(1)} %fourth_powers.1.powers) | copy-start | bytes 12582916
  95.5 33.0 %copy-start.1 = (s32[256]{0:T(256)S(1)}, s32[256]{0:T(256)}, u32[]{:S(2)}) copy-start(s32[256]{0:T(256)} %order.5) | copy-start | bytes 3076
  118.8 7.6 %collective-permute-start.2 = (bf16[32,8,512]{2,1,0:T(8,128)(2,1)S(1)}, bf16[32,8,512]{2,1,0:T(8,128)(2,1)S(1)}, u32[]{:S(2)}, u32[]{:S(2)}) collective-permute-start(bf16[32,8,512]{2,1,0:T(8,128)(2,1)S(1)} %get-tuple-element.6), channel_id=1, source_target_pairs={{0,192},{64,0},{128,64},{192,128},{1,193},{65,1},{129,65},{193,129... | collective-permute-start | bytes 786440 | tf_op jit(solution)/shard_map/ppermute | solution.py:254
  119.7 8.7 %collective-permute-start = (bf16[32,8,512]{2,1,0:T(8,128)(2,1)S(1)}, bf16[32,8,512]{2,1,0:T(8,128)(2,1)S(1)}, u32[]{:S(2)}, u32[]{:S(2)}) collective-permute-start(bf16[32,8,512]{2,1,0:T(8,128)(2,1)S(1)} %get-tuple-element.7), channel_id=1, source_target_pairs={{0,64},{64,128},{128,192},{192,0},{1,65},{65,129},{129,193},{193,1... | collective-permute-start | bytes 786440 | tf_op jit(solution)/shard_map/ppermute | solution.py:254
  120.3 13.4 %collective-permute-start.4 = (bf16[32,8,512]{2,1,0:T(8,128)(2,1)S(1)}, bf16[32,8,512]{2,1,0:T(8,128)(2,1)S(1)}, u32[]{:S(2)}, u32[]{:S(2)}) collective-permute-start(bf16[32,8,512]{2,1,0:T(8,128)(2,1)S(1)} %get-tuple-element.6), channel_id=1, source_target_pairs={{0,64},{64,128},{128,192},{192,0},{1,65},{65,129},{129,193},{193,1... | collective-permute-start | bytes 786440 | tf_op jit(solution)/shard_map/ppermute | solution.py:254
  120.6 13.1 %collective-permute-start.5 = (bf16[32,8,512]{2,1,0:T(8,128)(2,1)S(1)}, bf16[32,8,512]{2,1,0:T(8,128)(2,1)S(1)}, u32[]{:S(2)}, u32[]{:S(2)}) collective-permute-start(bf16[32,8,512]{2,1,0:T(8,128)(2,1)S(1)} %get-tuple-element.7), channel_id=1, source_target_pairs={{0,192},{64,0},{128,64},{192,128},{1,193},{65,1},{129,65},{193,129... | collective-permute-start | bytes 786440 | tf_op jit(solution)/shard_map/ppermute | solution.py:254
  126.3 11.2 %collective-permute-start.3 = (bf16[32,8,512]{2,1,0:T(8,128)(2,1)S(1)}, bf16[32,8,512]{2,1,0:T(8,128)(2,1)S(1)}, u32[]{:S(2)}, u32[]{:S(2)}) collective-permute-start(bf16[32,8,512]{2,1,0:T(8,128)(2,1)S(1)} %collective-permute-done.2.refs_2_), channel_id=1, source_target_pairs={{0,192},{64,0},{128,64},{192,128},{1,193},{65,1},{129,65},{193,129... | collective-permute-start | bytes 786440 | tf_op jit(solution)/shard_map/ppermute | solution.py:254
  128.4 10.9 %collective-permute-start.1 = (bf16[32,8,512]{2,1,0:T(8,128)(2,1)S(1)}, bf16[32,8,512]{2,1,0:T(8,128)(2,1)S(1)}, u32[]{:S(2)}, u32[]{:S(2)}) collective-permute-start(bf16[32,8,512]{2,1,0:T(8,128)(2,1)S(1)} %collective-permute-done.refs_1_), channel_id=1, source_target_pairs={{0,64},{64,128},{128,192},{192,0},{1,65},{65,129},{129,193},{193,1... | collective-permute-start | bytes 786440 | tf_op jit(solution)/shard_map/ppermute | solution.py:254
